TPU v7x, 512 devices: a whole 4x8x8 slice. The times are simulated.
512 devices in a mesh: chan: 8 (over x, core), filt: 16 (over z_lo, y), sp: 4 (over z_hi).
Axes of the slice: x: 4, y: 8, z: 8 (z_hi: 4, z_lo: 2; z = z_hi * 2 + z_lo), core: 2. Of those that a mesh axis runs over, the one named last changes fastest.
Arguments:
- activations: bfloat16 [512, 4, 2048], P('chan', 'sp', 'filt'), may hold values from -6 to 6
- weights: bfloat16 [3, 3, 3, 512, 512], P(None, None, None, 'chan', 'filt'), may hold values from -0.0546875 to 0.0546875
- out_grad: bfloat16 [512, 4, 2048], P('filt', 'sp', 'chan'), may hold values from -6 to 6
Outputs:
- responses: bfloat16 [512, 4, 2048], P('filt', 'sp', 'chan')
- in_grad: bfloat16 [512, 4, 2048], P('chan', 'sp', 'filt')
All inputs are finite; a program needn't handle non-finite values.
Results may differ from a plain program's by a relative error of at most 0.001.
Values may be sent and summed in bfloat16 or wider, within the bound.
A program may use at most 64 MiB of HBM per device.

v0:
```python
import jax
import jax.numpy as jnp
from jax import lax
from jax.sharding import PartitionSpec as P

Z = 64


def with_halo(cells, sides, width):
    for axis, dim in sides:
        count = lax.axis_size(axis)
        ends = count - 1
        head = lax.slice_in_dim(cells, 0, width, axis=dim)
        tail = lax.slice_in_dim(cells, cells.shape[dim] - width, cells.shape[dim], axis=dim)
        cells = jnp.concatenate(
            [
                lax.ppermute(tail, axis, [(i, (i + 1) % count) for i in range(ends)]),
                cells,
                lax.ppermute(head, axis, [((i + 1) % count, i) for i in range(ends)]),
            ],
            axis=dim,
        )
    return cells


def tap_list():
    return [
        (shift_x, shift_y, shift_z)
        for shift_x in range(3)
        for shift_y in range(3)
        for shift_z in range(3)
    ]


def forward_sum(padded, weights, count_x, count_y, count_z):
    total = jnp.zeros((weights.shape[4], count_x * count_y * count_z), jnp.float32)
    for shift_x, shift_y, shift_z in tap_list():
        window = lax.slice(
            padded,
            (0, shift_x, shift_y, shift_z),
            (padded.shape[0], shift_x + count_x, shift_y + count_y, shift_z + count_z),
        )
        window = window.reshape(padded.shape[0], -1)
        total = total + lax.dot_general(
            weights[shift_x, shift_y, shift_z],
            window,
            (((0,), (0,)), ((), ())),
            preferred_element_type=jnp.float32,
        )
    return total.reshape(-1, count_x, count_y * count_z)


def backward_sum(padded, weights, count_x, count_y, count_z):
    total = jnp.zeros((weights.shape[3], count_x * count_y * count_z), jnp.float32)
    for shift_x, shift_y, shift_z in tap_list():
        start_x, start_y, start_z = (2 - shift_x, 2 - shift_y, 2 - shift_z)
        window = lax.slice(
            padded,
            (0, start_x, start_y, start_z),
            (padded.shape[0], start_x + count_x, start_y + count_y, start_z + count_z),
        )
        window = window.reshape(padded.shape[0], -1)
        total = total + lax.dot_general(
            weights[shift_x, shift_y, shift_z],
            window,
            (((1,), (0,)), ((), ())),
            preferred_element_type=jnp.float32,
        )
    return total.reshape(-1, count_x, count_y * count_z)


def local(activations, weights, out_grad):
    count_x = activations.shape[1]
    depth = Z
    panels = lax.all_gather(activations, "filt", axis=2, tiled=True)
    panels = panels.reshape(panels.shape[0], count_x, -1, depth)
    rimmed = with_halo(panels, (("sp", 1),), 1)
    padded = jnp.pad(rimmed, ((0, 0), (0, 0), (1, 1), (1, 1)))
    partial_value = forward_sum(padded, weights, count_x, panels.shape[2], depth)
    responses = lax.psum_scatter(partial_value, "chan", scatter_dimension=2, tiled=True).astype(
        jnp.bfloat16
    )
    grad_panels = lax.all_gather(out_grad, "chan", axis=2, tiled=True)
    grad_block = grad_panels.reshape(grad_panels.shape[0], count_x, -1, depth)
    grad_rimmed = with_halo(grad_block, (("sp", 1),), 1)
    grad_padded = jnp.pad(grad_rimmed, ((0, 0), (0, 0), (1, 1), (1, 1)))
    grad_part = backward_sum(grad_padded, weights, count_x, grad_block.shape[2], depth)
    in_grad = lax.psum_scatter(grad_part, "filt", scatter_dimension=2, tiled=True).astype(
        jnp.bfloat16
    )
    return (responses, in_grad)


def solution(mesh):
    return jax.shard_map(
        local,
        mesh=mesh,
        in_specs=(
            P("chan", "sp", "filt"),
            P(None, None, None, "chan", "filt"),
            P("filt", "sp", "chan"),
        ),
        out_specs=(P("filt", "sp", "chan"), P("chan", "sp", "filt")),
        check_vma=False,
    )
```

profile of v0, /device:TPU:4, one launch (start us, length us, event | category | flops | bytes accessed | tf_op | source)
XLA Modules:
  0.0 385.1 jit_solution(1077133087643198537)
XLA Ops:
  7.2 16.8 %all_gather.7 = bf16[32,1,2048]{2,0,1:T(8,128)(2,1)S(1)} all-gather(bf16[32,1,256]{2,0,1:T(8,128)(2,1)} %param.5), channel_id=1, replica_groups=mesh['chan'=8,'filt'=16,'sp'=4] {'chan'}, dimensions={2}, use_global_device_ids=true | all-gather | bytes 147456 | tf_op jit(solution)/shard_map/all_gather | solution.py:83
  25.6 5.5 %collective-permute-start.2 = (bf16[32,1,32,64]{3,2,0,1:T(8,128)(2,1)S(1)}, bf16[32,1,32,64]{3,2,0,1:T(8,128)(2,1)S(1)}, u32[]{:S(2)}, u32[]{:S(2)}) collective-permute-start(bf16[32,1,32,64]{3,2,0,1:T(8,128)(2,1)S(1)} %reshape.209), channel_id=1, source_target_pairs={{0,1},{1,2},{2,3},{4,5},{5,6},{6,7},{8,9},{9,10},{10,11},{12,13},{... | collective-permute-start | bytes 393224 | tf_op jit(solution)/shard_map/ppermute | solution.py:17
  31.0 32.7 %all_gather.6 = bf16[64,1,2048]{2,0,1:T(8,128)(2,1)S(1)} all-gather(bf16[64,1,128]{2,0,1:T(8,128)(2,1)} %param.3), channel_id=1, replica_groups=mesh['chan'=8,'filt'=16,'sp'=4] {'filt'}, dimensions={2}, use_global_device_ids=true | all-gather | bytes 278528 | tf_op jit(solution)/shard_map/all_gather | solution.py:75
  66.3 7.5 %collective-permute-start = (bf16[64,1,32,64]{3,2,0,1:T(8,128)(2,1)}, bf16[64,1,32,64]{3,2,0,1:T(8,128)(2,1)S(1)}, u32[]{:S(2)}, u32[]{:S(2)}) collective-permute-start(bf16[64,1,32,64]{3,2,0,1:T(8,128)(2,1)} %reshape.180), channel_id=1, source_target_pairs={{0,1},{1,2},{2,3},{4,5},{5,6},{6,7},{8,9},{9,10},{10,11},{12,13},{... | collective-permute-start | bytes 786440 | tf_op jit(solution)/shard_map/ppermute | solution.py:17
  76.4 3.2 fusion.172
  151.6 3.3 fusion.11
  160.1 2.9 select_maximum_fusion
  165.0 4.9 %fusion.170 = (bf16[64,1,32,64]{3,2,0,1:T(8,128)(2,1)}, bf16[64,1,32,64]{3,2,0,1:T(8,128)(2,1)}, bf16[64,1,32,64]{3,2,0,1:T(8,128)(2,1)}, bf16[64,1,32,64]{3,2,0...) fusion(bf16[64,3,34,66]{3,2,0,1:T(8,128)(2,1)S(1)} %select_maxi, ...), kind=kLoop, calls=%fused_computation.233 | loop fusion | bytes 9961472 | tf_op jit(solution)/shard_map/slice | solution.py:38
  171.3 2.2 reshape.183
  173.5 2.2 reshape.182
  175.8 2.2 reshape.181
  179.8 2.2 reshape.207
  183.9 2.2 reshape.206
  186.1 2.2 reshape.205
  198.2 2.2 reshape.201
  202.2 2.2 reshape.200
  206.2 2.2 reshape.199
  210.3 2.2 reshape.198
  214.3 2.2 reshape.197
  218.4 2.2 reshape.196
  222.5 2.2 reshape.195
  226.6 2.2 reshape.193
  230.6 2.2 reshape.192
  234.7 2.2 reshape.191
  238.8 2.2 reshape.190
  246.8 2.2 reshape.188
  249.0 2.2 reshape.187
  253.1 2.2 reshape.186
  262.8 2.4 fusion.39
  269.7 2.6 fusion.19
  274.1 22.9 %reduce-scatter.3.cloned.1.call-done = f32[32,1,256]{2,0,1:T(8,128)} async-done(((f32[32,1,2048]{2,0,1:T(8,128)}), f32[32,1,256]{2,0,1:T(8,128)}) %reduce-scatter.3.cloned.1.call-update) | async-done | bytes 32784 | tf_op jit(solution)/shard_map/reduce_scatter | solution.py:80
  298.4 78.5 %reduce-scatter.5.cloned.1.call-done = f32[64,1,128]{2,0,1:T(8,128)} async-done(((f32[64,1,2048]{2,0,1:T(8,128)}), f32[64,1,128]{2,0,1:T(8,128)}) %reduce-scatter.5.cloned.1.call-update) | async-done | bytes 32784 | tf_op jit(solution)/shard_map/reduce_scatter | solution.py:88
  (140 shorter events, 143.6 us)
Async XLA Ops:
  7.2 289.9 %reduce-scatter.3.cloned.1.call-start = ((), (), s32[]{:S(2)}) async-start(), calls=%async_computation.2 | async-start | bytes 294912 | tf_op jit(solution)/shard_map/reduce_scatter | solution.py:80
  24.3 51.1 %collective-permute-start.3 = (bf16[32,1,32,64]{3,2,0,1:T(8,128)(2,1)S(1)}, bf16[32,1,32,64]{3,2,0,1:T(8,128)(2,1)S(1)}, u32[]{:S(2)}, u32[]{:S(2)}) collective-permute-start(bf16[32,1,32,64]{3,2,0,1:T(8,128)(2,1)S(1)} %reshape.209), channel_id=1, source_target_pairs={{1,0},{2,1},{3,2},{5,4},{6,5},{7,6},{9,8},{10,9},{11,10},{13,12},{... | collective-permute-start | bytes 393224 | tf_op jit(solution)/shard_map/ppermute | solution.py:19
  25.6 49.8 %collective-permute-start.2 = (bf16[32,1,32,64]{3,2,0,1:T(8,128)(2,1)S(1)}, bf16[32,1,32,64]{3,2,0,1:T(8,128)(2,1)S(1)}, u32[]{:S(2)}, u32[]{:S(2)}) collective-permute-start(bf16[32,1,32,64]{3,2,0,1:T(8,128)(2,1)S(1)} %reshape.209), channel_id=1, source_target_pairs={{0,1},{1,2},{2,3},{4,5},{5,6},{6,7},{8,9},{9,10},{10,11},{12,13},{... | collective-permute-start | bytes 393224 | tf_op jit(solution)/shard_map/ppermute | solution.py:17
  65.0 95.0 %collective-permute-start.1 = (bf16[64,1,32,64]{3,2,0,1:T(8,128)(2,1)}, bf16[64,1,32,64]{3,2,0,1:T(8,128)(2,1)S(1)}, u32[]{:S(2)}, u32[]{:S(2)}) collective-permute-start(bf16[64,1,32,64]{3,2,0,1:T(8,128)(2,1)} %reshape.180), channel_id=1, source_target_pairs={{1,0},{2,1},{3,2},{5,4},{6,5},{7,6},{9,8},{10,9},{11,10},{13,12},{... | collective-permute-start | bytes 786440 | tf_op jit(solution)/shard_map/ppermute | solution.py:19
  66.3 93.7 %collective-permute-start = (bf16[64,1,32,64]{3,2,0,1:T(8,128)(2,1)}, bf16[64,1,32,64]{3,2,0,1:T(8,128)(2,1)S(1)}, u32[]{:S(2)}, u32[]{:S(2)}) collective-permute-start(bf16[64,1,32,64]{3,2,0,1:T(8,128)(2,1)} %reshape.180), channel_id=1, source_target_pairs={{0,1},{1,2},{2,3},{4,5},{5,6},{6,7},{8,9},{9,10},{10,11},{12,13},{... | collective-permute-start | bytes 786440 | tf_op jit(solution)/shard_map/ppermute | solution.py:17
  75.3 1.1 copy-start.1
  117.1 8.9 %copy-start.18 = (bf16[32,2048]{1,0:T(8,128)(2,1)S(1)}, bf16[32,2048]{1,0:T(8,128)(2,1)}, u32[]{:S(2)}) copy-start(bf16[32,2048]{1,0:T(8,128)(2,1)} %reshape.220) | copy-start | bytes 393220
  117.1 10.7 %copy-start.17 = (bf16[32,2048]{1,0:T(8,128)(2,1)S(1)}, bf16[32,2048]{1,0:T(8,128)(2,1)}, u32[]{:S(2)}) copy-start(bf16[32,2048]{1,0:T(8,128)(2,1)} %reshape.221) | copy-start | bytes 393220
  118.0 6.1 %copy-start.19 = (bf16[32,2048]{1,0:T(8,128)(2,1)S(1)}, bf16[32,2048]{1,0:T(8,128)(2,1)}, u32[]{:S(2)}) copy-start(bf16[32,2048]{1,0:T(8,128)(2,1)} %reshape.219) | copy-start | bytes 393220
  118.0 11.6 %copy-start.16 = (bf16[32,2048]{1,0:T(8,128)(2,1)S(1)}, bf16[32,2048]{1,0:T(8,128)(2,1)}, u32[]{:S(2)}) copy-start(bf16[32,2048]{1,0:T(8,128)(2,1)} %reshape.222) | copy-start | bytes 393220
  120.0 11.3 %copy-start.15 = (bf16[32,2048]{1,0:T(8,128)(2,1)S(1)}, bf16[32,2048]{1,0:T(8,128)(2,1)}, u32[]{:S(2)}) copy-start(bf16[32,2048]{1,0:T(8,128)(2,1)} %reshape.224) | copy-start | bytes 393220
  122.1 11.1 %copy-start.14 = (bf16[32,2048]{1,0:T(8,128)(2,1)S(1)}, bf16[32,2048]{1,0:T(8,128)(2,1)}, u32[]{:S(2)}) copy-start(bf16[32,2048]{1,0:T(8,128)(2,1)} %reshape.225) | copy-start | bytes 393220
  124.1 10.9 %copy-start.13 = (bf16[32,2048]{1,0:T(8,128)(2,1)S(1)}, bf16[32,2048]{1,0:T(8,128)(2,1)}, u32[]{:S(2)}) copy-start(bf16[32,2048]{1,0:T(8,128)(2,1)} %reshape.226) | copy-start | bytes 393220
  125.9 10.9 %copy-start.12 = (bf16[32,2048]{1,0:T(8,128)(2,1)S(1)}, bf16[32,2048]{1,0:T(8,128)(2,1)}, u32[]{:S(2)}) copy-start(bf16[32,2048]{1,0:T(8,128)(2,1)} %reshape.227) | copy-start | bytes 393220
  127.7 10.9 %copy-start.11 = (bf16[32,2048]{1,0:T(8,128)(2,1)S(1)}, bf16[32,2048]{1,0:T(8,128)(2,1)}, u32[]{:S(2)}) copy-start(bf16[32,2048]{1,0:T(8,128)(2,1)} %reshape.228) | copy-start | bytes 393220
  129.6 10.8 %copy-start.10 = (bf16[32,2048]{1,0:T(8,128)(2,1)S(1)}, bf16[32,2048]{1,0:T(8,128)(2,1)}, u32[]{:S(2)}) copy-start(bf16[32,2048]{1,0:T(8,128)(2,1)} %reshape.229) | copy-start | bytes 393220
  131.4 10.8 %copy-start.9 = (bf16[32,2048]{1,0:T(8,128)(2,1)S(1)}, bf16[32,2048]{1,0:T(8,128)(2,1)}, u32[]{:S(2)}) copy-start(bf16[32,2048]{1,0:T(8,128)(2,1)} %reshape.230) | copy-start | bytes 393220
  133.2 10.8 %copy-start.8 = (bf16[32,2048]{1,0:T(8,128)(2,1)S(1)}, bf16[32,2048]{1,0:T(8,128)(2,1)}, u32[]{:S(2)}) copy-start(bf16[32,2048]{1,0:T(8,128)(2,1)} %reshape.231) | copy-start | bytes 393220
  135.0 10.8 %copy-start.7 = (bf16[32,2048]{1,0:T(8,128)(2,1)S(1)}, bf16[32,2048]{1,0:T(8,128)(2,1)}, u32[]{:S(2)}) copy-start(bf16[32,2048]{1,0:T(8,128)(2,1)} %reshape.233) | copy-start | bytes 393220
  136.8 9.9 %copy-start.4 = (bf16[32,2048]{1,0:T(8,128)(2,1)S(1)}, bf16[32,2048]{1,0:T(8,128)(2,1)}, u32[]{:S(2)}) copy-start(bf16[32,2048]{1,0:T(8,128)(2,1)} %reshape.211) | copy-start | bytes 393220
  140.4 7.3 %copy-start.3 = (bf16[32,2048]{1,0:T(8,128)(2,1)S(1)}, bf16[32,2048]{1,0:T(8,128)(2,1)}, u32[]{:S(2)}) copy-start(bf16[32,2048]{1,0:T(8,128)(2,1)} %reshape.212) | copy-start | bytes 393220
  144.0 4.7 %copy-start.5 = (bf16[32,2048]{1,0:T(8,128)(2,1)S(1)}, bf16[32,2048]{1,0:T(8,128)(2,1)}, u32[]{:S(2)}) copy-start(bf16[32,2048]{1,0:T(8,128)(2,1)} %reshape.213) | copy-start | bytes 393220
  151.6 3.3 copy-start.6
  265.2 4.5 %copy-start = (f32[64,2048]{1,0:T(8,128)S(1)}, f32[64,2048]{1,0:T(8,128)}, u32[]{:S(2)}) copy-start(f32[64,2048]{1,0:T(8,128)} %convolution_bitcast_fusion.11) | copy-start | bytes 1572868
  269.6 2.6 copy-start.2
  269.6 107.3 %reduce-scatter.5.cloned.1.call-start = ((), (), s32[]{:S(2)}) async-start(), calls=%async_computation.3 | async-start | bytes 557056 | tf_op jit(solution)/shard_map/reduce_scatter | solution.py:88
Sparse Core Ops, SparseCore 0:
  269.7 27.2 reduce-scatter.2
  300.0 76.8 reduce-scatter.4
where the time goes:
time: 388 us; the launch traced here: 385 us
  local copies, waits for them, and re-layouts  106 us (27%)
  waiting for transfers between devices  102 us (26%)
  matrix products  91.8 us (24%)
  blocking collectives  49.5 us (13%)
  starting transfers between devices  15.6 us (4%)
  between operations  14.3 us (4%)
  other arithmetic  6.3 us (2%)
    reduce_scatter x1, waiting for transfers between devices, local(): lax.psum_scatter(grad_part, 'filt', scatter_dimension=2, tiled=True)  78.5 us
    reshape x26, local copies, waits for them, and re-layouts, forward_sum(): window = window.reshape(padded.shape[0], -1)  53.9 us
    dot_general x27, matrix products, forward_sum(): lax.dot_general(weights[shift_x, shift_y, shift_z], window, (((0,), (0,))...  47.4 us
    dot_general x27, matrix products, backward_sum(): lax.dot_general(weights[shift_x, shift_y, shift_z], window, (((1,), (0,))...  44.5 us
    reshape x26, local copies, waits for them, and re-layouts, backward_sum(): window = window.reshape(padded.shape[0], -1)  40.1 us
    all_gather x1, blocking collectives, local(): panels = lax.all_gather(activations, 'filt', axis=2, tiled=True)  32.7 us
    reduce_scatter x1, waiting for transfers between devices, local(): lax.psum_scatter(partial_value, 'chan', scatter_dimension=2, tiled=True)  22.9 us
    all_gather x1, blocking collectives, local(): grad_panels = lax.all_gather(out_grad, 'chan', axis=2, tiled=True)  16.8 us
  transfers between devices with their start and end apart: 6, of which 2 were waited for; matrix products, arithmetic and copies ran while one was open for 24% of the time, Pallas kernels for 0%

commit v1 on v0

v1 whole, which is shorter than its diff:
```python
import functools

import jax
import jax.numpy as jnp
from jax import lax
from jax.experimental import pallas as pl
from jax.experimental.pallas import tpu as pltpu
from jax.sharding import PartitionSpec as P

MESH = pl.DeviceIdType.MESH
BF16 = jnp.bfloat16
F32 = jnp.float32
B = 32
LANES = 128


def kernel(
    nx, ny, ns,
    act_ref, w_hbm, og_ref, resp_ref, grad_ref,
    w_ref, d_ref, g_ref, hd_ref, hg_ref, wr_ref, lf_ref, lb_ref, r_ref,
    pb_ref, pf_ref, rb_ref, rf_ref,
    w_sem, loc_sem, f1_send, f1_recv, f2_send, f2_recv, b1_send, b1_recv, b2_send, b2_recv,
    ws_send, ws_recv, h_send, h_recv, b3_send, b3_recv, f3_send, f3_recv,
):
    xh = nx // 2
    tpb = ny // nx
    chan, filt, s = lax.axis_index("chan"), lax.axis_index("filt"), lax.axis_index("sp")
    x, core = chan // 2, chan % 2
    zl, y = filt // ny, filt % ny
    k, xi = x // xh, x % xh
    other = 1 - core
    first, last = s == 0, s == ns - 1
    inner = jnp.logical_and(s > 0, s < ns - 1)
    relay = core == k

    def dev(x_, core_, zl_, y_, s_):
        return (x_ * 2 + core_, zl_ * ny + y_, s_)

    def remote(src, dst, ssem, rsem, to):
        return pltpu.make_async_remote_copy(
            src_ref=src, dst_ref=dst, send_sem=ssem, recv_sem=rsem,
            device_id=to, device_id_type=MESH,
        )

    def on_slabs(body):
        pl.when(s > 0)(lambda: body(-1))
        pl.when(s < ns - 1)(lambda: body(1))
        body(0)

    load = pltpu.make_async_copy(w_hbm, w_ref, w_sem)
    load.start()

    barrier = pltpu.get_barrier_semaphore()

    def greet(to):
        pl.semaphore_signal(barrier, inc=1, device_id=to, device_id_type=MESH)

    def greet_slab(ds):
        for dc in range(2):
            for dz in range(2):
                if (ds, dc, dz) != (0, 0, 0):
                    greet(dev(x, (core + dc) % 2, (zl + dz) % 2, y, s + ds))

    on_slabs(greet_slab)
    for d in range(1, ny):
        greet(dev(x, core, zl, (y + d) % ny, s))
        for zs in range(2):
            greet(dev(x, zl, zs, (y + d) % ny, s))
    for d in range(1, nx):
        greet(dev((x + d) % nx, core, zl, y, s))

    def clear_planes(p):
        d_ref[y, p] = jnp.zeros(d_ref.shape[2:], BF16)

        @pl.when(relay)
        def _():
            for c in range(2):
                g_ref[xi, c, p] = jnp.zeros(g_ref.shape[3:], BF16)

    pl.when(first)(lambda: clear_planes(0))
    pl.when(last)(lambda: clear_planes(2))

    peers = 3 + 3 * (ny - 1) + (nx - 1)
    pl.semaphore_wait(barrier, peers + 8 - 4 * first.astype(jnp.int32) - 4 * last.astype(jnp.int32))

    def f1_copy(ds, dz):
        z2 = (zl + dz) % 2
        return (
            act_ref.at[pl.ds(z2 * B, B), :],
            d_ref.at[y, 1 - ds, pl.ds(core * B, B), :],
            f1_send.at[ds + 1, dz], f1_recv, dev(x, zl, z2, y, s + ds),
        )

    def b1_copy(ds, dz):
        z2 = (zl + dz) % 2
        return (
            og_ref,
            g_ref.at[xi, core, 1 - ds, pl.ds(zl * B, B), :],
            b1_send.at[ds + 1, dz], b1_recv, dev(x, k, z2, y, s + ds),
        )

    def start(args, own):
        if own is None:
            remote(*args).start()
            return
        pl.when(jnp.logical_not(own))(lambda: remote(*args).start())
        pl.when(own)(lambda: pltpu.make_async_copy(args[0], args[1], args[3]).start())

    def finish(args, own):
        if own is None:
            remote(*args).wait_send()
        else:
            pl.when(jnp.logical_not(own))(lambda: remote(*args).wait_send())

    def first_sends(act):
        def slab(ds):
            for dz in range(2):
                here = (ds, dz) == (0, 0)
                act(f1_copy(ds, dz), (core == zl) if here else None)
                act(b1_copy(ds, dz), relay if here else None)

        on_slabs(slab)

    first_sends(start)

    load.wait()
    blank = jnp.zeros((B, B), BF16)
    for a in range(3):
        for e in range(3):
            taps = [w_ref[a * 9 + b * 3 + e] for b in range(3)]
            for h in range(2):
                slot = jnp.where(zl == h, h, 2)
                fwd = jnp.concatenate([t[:, h * B:(h + 1) * B] for t in taps] + [blank], axis=1)
                flip = fwd.astype(F32).T
                bwd = jnp.concatenate([flip[(2 - b) * B:(3 - b) * B] for b in range(3)] + [flip[3 * B:]], axis=1)
                wr_ref[core, slot, 0, a * 3 + e] = fwd
                wr_ref[core, slot, 1, a * 3 + e] = bwd.astype(BF16)
    w_across = (wr_ref.at[core, 2], wr_ref.at[core, zl], ws_send.at[0], ws_recv.at[0], dev(x, core, 1 - zl, y, s))
    w_own = (wr_ref.at[core, zl], wr_ref.at[core, zl], ws_send.at[1], ws_recv.at[1], dev(x, other, zl, y, s))
    w_next = (wr_ref.at[core, 1 - zl], wr_ref.at[core, 1 - zl], ws_send.at[2], ws_recv.at[2], dev(x, other, zl, y, s))
    remote(*w_across).start()
    remote(*w_own).start()

    def wait_planes(whole, low, high, sem):
        pl.when(inner)(lambda: pltpu.make_async_copy(whole, whole, sem).wait())
        pl.when(first)(lambda: pltpu.make_async_copy(high, high, sem).wait())
        pl.when(last)(lambda: pltpu.make_async_copy(low, low, sem).wait())

    wait_planes_f1 = functools.partial(
        wait_planes, d_ref.at[y], d_ref.at[y, pl.ds(0, 2)], d_ref.at[y, pl.ds(1, 2)], f1_recv)

    def b2_copy(d):
        return (g_ref.at[xi], g_ref.at[xi], b2_send.at[d - 1], b2_recv.at[xi], dev((x + d) % nx, core, zl, y, s))

    def f2_copy(d):
        return (d_ref.at[y], d_ref.at[y], f2_send.at[d - 1], f2_recv.at[y], dev(x, core, zl, (y + d) % ny, s))

    wait_planes_f1()
    for d in range(1, ny):
        remote(*f2_copy(d)).start()

    @pl.when(relay)
    def _():
        wait_planes(g_ref.at[xi], g_ref.at[xi, :, pl.ds(0, 2)], g_ref.at[xi, :, pl.ds(1, 2)], b1_recv)
        for d in range(1, nx):
            remote(*b2_copy(d)).start()

    remote(*w_across).wait_recv()
    remote(*w_next).start()

    def halo_g(src_x, src_c, lane):
        return (g_ref.at[src_x, src_c, :, :, pl.ds(lane, LANES)], hg_ref, h_send.at[0], h_recv.at[0],
                dev(x, other, zl, y, s))

    def halo_d(src_y):
        return (d_ref.at[src_y], hd_ref, h_send.at[1], h_recv.at[1], dev(x, other, zl, y, s))

    for i in range(xh):
        @pl.when(jnp.logical_not(jnp.logical_and(relay, xi == i)))
        def _(i=i):
            pltpu.make_async_copy(g_ref.at[i], g_ref.at[i], b2_recv.at[i]).wait()

    low_g = halo_g(0, 0, 0)
    high_g = halo_g(xh - 1, 1, (tpb - 1) * LANES)
    pl.when(core == 0)(lambda: remote(*high_g).start())
    pl.when(core == 1)(lambda: remote(*low_g).start())

    remote(*w_own).wait_recv()
    remote(*w_next).wait_recv()
    for cs in range(2):
        for z in range(2):
            for a in range(3):
                for e in range(3):
                    lf_ref[e * 64 + z * B:e * 64 + z * B + B, a * 256 + cs * 128:a * 256 + cs * 128 + 128] = (
                        wr_ref[cs, z, 0, a * 3 + e])
                    lb_ref[e * 64 + cs * B:e * 64 + cs * B + B, a * 256 + z * 128:a * 256 + z * 128 + 128] = (
                        wr_ref[cs, z, 1, (2 - a) * 3 + 2 - e])
    for a in range(3):
        for c in range(2):
            row = a * 256 + c * 128 + 96
            r_ref[row:row + B, :] = jnp.zeros((B, r_ref.shape[1]), BF16)

    lane = lax.broadcasted_iota(jnp.int32, (64, LANES), 1)
    left_half = lane < 64
    inside_low = lane % 64 != 0
    inside_high = lane % 64 != 63

    def put(a, b, t, tile):
        for c in range(2):
            row = a * 256 + c * 128 + b * B
            r_ref[row:row + B, t * LANES:(t + 1) * LANES] = tile[c * B:(c + 1) * B]

    def rows(tile_of, halo_of):
        for a in range(3):
            halo = halo_of(a)
            none = jnp.zeros_like(halo)
            tiles = [jnp.where(core == 1, halo, none)]
            tiles += [tile_of(a, t) for t in range(ny)]
            tiles += [jnp.where(core == 0, halo, none)]
            turned = [pltpu.roll(t.astype(F32), 64, axis=1) for t in tiles]
            for t in range(ny + 1):
                mid = jnp.where(left_half, turned[t], turned[t + 1]).astype(BF16)
                if t < ny:
                    put(a, 0, t, mid)
                    put(a, 1, t, tiles[t + 1])
                if t > 0:
                    put(a, 2, t - 1, mid)

    def multiply(l_ref, emit):
        for pair in range(ny // 2):
            part = jnp.dot(l_ref[...], r_ref[:, pair * 256:(pair + 1) * 256], preferred_element_type=F32)
            for h in range(2):
                piece = part[:, h * LANES:(h + 1) * LANES]
                total = piece[64:128]
                total += jnp.where(inside_low, pltpu.roll(piece[0:64], 1, axis=1), 0.0)
                total += jnp.where(inside_high, pltpu.roll(piece[128:192], LANES - 1, axis=1), 0.0)
                emit(pair * 2 + h, total)

    pl.when(core == 0)(lambda: remote(*low_g).wait_recv())
    pl.when(core == 1)(lambda: remote(*high_g).wait_recv())

    def g_tile(a, t):
        j, h = t // tpb, t % tpb
        return g_ref[j // 2, j % 2, a, :, h * LANES:(h + 1) * LANES]

    rows(g_tile, lambda a: hg_ref[a])

    def emit_b(t, total):
        pb_ref[t] = total

    multiply(lb_ref, emit_b)

    def b3_copy(d, dc):
        y2, c2 = (y + d) % ny, (core + dc) % 2
        return (
            pb_ref.at[y2, pl.ds(c2 * B, B), :],
            rb_ref.at[y, pl.ds(zl * B, B), :],
            b3_send.at[d, dc], b3_recv, dev(x, c2, core, y2, s),
        )

    def b3_sends(act):
        for d in range(ny):
            for dc in range(2):
                act(b3_copy(d, dc), (core == zl) if (d, dc) == (0, 0) else None)

    b3_sends(start)

    for d in range(1, ny):
        y2 = (y + d) % ny
        pltpu.make_async_copy(d_ref.at[y2], d_ref.at[y2], f2_recv.at[y2]).wait()
    low_d = halo_d(0)
    high_d = halo_d(ny - 1)
    pl.when(core == 0)(lambda: remote(*high_d).start())
    pl.when(core == 1)(lambda: remote(*low_d).start())
    pl.when(core == 0)(lambda: remote(*low_d).wait_recv())
    pl.when(core == 1)(lambda: remote(*high_d).wait_recv())
    rows(lambda a, t: d_ref[t, a], lambda a: hd_ref[a])

    def emit_f(t, total):
        j, h = t // tpb, t % tpb
        for z in range(2):
            pf_ref[j, z, :, h * LANES:(h + 1) * LANES] = total[z * B:(z + 1) * B]

    multiply(lf_ref, emit_f)

    def f3_copy(j, dz):
        x2, c2, z2 = core * xh + j // 2, j % 2, (zl + dz) % 2
        return (
            pf_ref.at[j, z2], rf_ref.at[x, zl], f3_send.at[j, dz], f3_recv, dev(x2, c2, z2, y, s),
        ), jnp.logical_and(x2 == x, c2 == core)

    def f3_sends(act):
        for j in range(nx):
            for dz in range(2):
                copy, own = f3_copy(j, dz)
                act(copy, own if dz == 0 else None)

    f3_sends(start)

    pltpu.make_async_copy(rb_ref, rb_ref, b3_recv).wait()
    total = rb_ref[0]
    for i in range(1, ny):
        total += rb_ref[i]
    grad_ref[...] = total.astype(BF16)

    pltpu.make_async_copy(rf_ref, rf_ref, f3_recv).wait()
    total = rf_ref[0, 0]
    for i in range(1, nx * 2):
        total += rf_ref[i // 2, i % 2]
    resp_ref[...] = total.astype(BF16)

    first_sends(finish)
    for copy in (w_across, w_own, w_next):
        remote(*copy).wait_send()
    for d in range(1, ny):
        remote(*f2_copy(d)).wait_send()

    @pl.when(relay)
    def _():
        for d in range(1, nx):
            remote(*b2_copy(d)).wait_send()

    pl.when(core == 0)(lambda: remote(*high_g).wait_send())
    pl.when(core == 1)(lambda: remote(*low_g).wait_send())
    pl.when(core == 0)(lambda: remote(*high_d).wait_send())
    pl.when(core == 1)(lambda: remote(*low_d).wait_send())
    b3_sends(finish)
    f3_sends(finish)


def solution(mesh):
    nx, ny, ns = mesh.shape["chan"] // 2, mesh.shape["filt"] // 2, mesh.shape["sp"]
    xh = nx // 2

    def local(activations, weights, out_grad):
        act = activations.reshape(2 * B, LANES)
        grad = out_grad.reshape(B, -1)
        wide = grad.shape[1]
        w = jnp.swapaxes(weights, 3, 4).reshape(27, B, 2 * B)
        dma = pltpu.SemaphoreType.DMA
        responses, in_grad = pl.pallas_call(
            functools.partial(kernel, nx, ny, ns),
            out_shape=(
                jax.ShapeDtypeStruct((B, wide), BF16),
                jax.ShapeDtypeStruct((2 * B, LANES), BF16),
            ),
            in_specs=[
                pl.BlockSpec(memory_space=pltpu.VMEM),
                pl.BlockSpec(memory_space=pl.ANY),
                pl.BlockSpec(memory_space=pltpu.VMEM),
            ],
            out_specs=(pl.BlockSpec(memory_space=pltpu.VMEM),) * 2,
            scratch_shapes=[
                pltpu.VMEM((27, B, 2 * B), BF16),
                pltpu.VMEM((ny, 3, 2 * B, LANES), BF16),
                pltpu.VMEM((xh, 2, 3, 2 * B, wide), BF16),
                pltpu.VMEM((3, 2 * B, LANES), BF16),
                pltpu.VMEM((3, 2 * B, LANES), BF16),
                pltpu.VMEM((2, 3, 2, 9, B, LANES), BF16),
                pltpu.VMEM((192, 768), BF16),
                pltpu.VMEM((192, 768), BF16),
                pltpu.VMEM((768, ny * LANES), BF16),
                pltpu.VMEM((ny, 2 * B, LANES), F32),
                pltpu.VMEM((nx, 2, B, wide), F32),
                pltpu.VMEM((ny, 2 * B, LANES), F32),
                pltpu.VMEM((nx, 2, B, wide), F32),
                dma, dma,
                dma((3, 2)), dma,
                dma((ny - 1,)), dma((ny,)),
                dma((3, 2)), dma,
                dma((nx - 1,)), dma((xh,)),
                dma((3,)), dma((3,)),
                dma((2,)), dma((2,)),
                dma((ny, 2)), dma,
                dma((nx, 2)), dma,
            ],
            compiler_params=pltpu.CompilerParams(
                collective_id=0, has_side_effects=True, vmem_limit_bytes=32 * 1024 * 1024,
            ),
        )(act, w, grad)
        return responses.reshape(out_grad.shape), in_grad.reshape(activations.shape)

    return jax.shard_map(
        local,
        mesh=mesh,
        in_specs=(
            P("chan", "sp", "filt"),
            P(None, None, None, "chan", "filt"),
            P("filt", "sp", "chan"),
        ),
        out_specs=(P("filt", "sp", "chan"), P("chan", "sp", "filt")),
        check_vma=False,
    )
```

time: 388 us -> 42.2 us (0.11)
  the two profiles are of different devices: /device:TPU:4 before, /device:TPU:1 now
where the time goes in v1:
time: 42.2 us; the launch traced here: 41.9 us
  Pallas kernels  37.7 us (89%)
  local copies, waits for them, and re-layouts  3.58 us (8%)
  between operations  0.65 us (2%)
    pallas_call x1, Pallas kernels, local(): pl.pallas_call(functools.partial(kernel, nx, ny, ns), out_shape=(jax.Shap...  37.7 us
    unnamed x8, local copies, waits for them, and re-layouts  3.58 us

profile of v1, /device:TPU:1, one launch (start us, length us, event | category | flops | bytes accessed | tf_op | source)
XLA Modules:
  0.0 41.9 jit_solution(5152550206268509616)
XLA Ops:
  0.6 0.0 copy-start
  0.6 0.9 %copy-done = bf16[3,3,3,64,32]{3,4,2,1,0:T(8,128)(2,1)S(1)} copy-done((bf16[3,3,3,64,32]{3,4,2,1,0:T(8,128)(2,1)S(1)}, bf16[3,3,3,64,32]{3,4,2,1,0:T(8,128)(2,1)}, u32[]{:S(2)}) %copy-start) | copy-done | bytes 110616
  1.6 0.0 copy-start.1
  1.6 0.7 %copy-done.1 = bf16[64,1,128]{2,0,1:T(8,128)(2,1)S(1)} copy-done((bf16[64,1,128]{2,0,1:T(8,128)(2,1)S(1)}, bf16[64,1,128]{2,0,1:T(8,128)(2,1)}, u32[]{:S(2)}) %copy-start.1) | copy-done | bytes 16408
  2.3 0.0 copy-start.2
  2.3 0.7 %copy-done.2 = bf16[32,1,256]{2,0,1:T(8,128)(2,1)S(1)} copy-done((bf16[32,1,256]{2,0,1:T(8,128)(2,1)S(1)}, bf16[32,1,256]{2,0,1:T(8,128)(2,1)}, u32[]{:S(2)}) %copy-start.2) | copy-done | bytes 16408
  3.0 37.7 %shard_map.50 = (bf16[32,256]{1,0:T(8,128)(2,1)S(1)}, bf16[64,128]{1,0:T(8,128)(2,1)S(1)}) custom-call(bf16[64,128]{1,0:T(8,128)(2,1)S(1)} %bitcast.8, bf16[27,32,64]{2,1,0:T(8,128)(2,1)S(1)} %bitcast.7, bf16[32,256]{1,0:T(8,128)(2,1)S(1)} %bitcast.9), custom_call_target="tpu_custom_call" | custom-call | tf_op jit(solution)/shard_map/pallas_call | solution.py:341
  40.7 0.6 %copy.7 = bf16[32,1,256]{2,0,1:T(8,128)(2,1)} copy(bf16[32,1,256]{2,0,1:T(8,128)(2,1)S(1)} %bitcast.11) | data formatting | bytes 32768
  41.3 0.6 %copy.8 = bf16[64,1,128]{2,0,1:T(8,128)(2,1)} copy(bf16[64,1,128]{2,0,1:T(8,128)(2,1)S(1)} %bitcast.10) | data formatting | bytes 32768
Async XLA Ops:
  0.6 0.9 %copy-start = (bf16[3,3,3,64,32]{3,4,2,1,0:T(8,128)(2,1)S(1)}, bf16[3,3,3,64,32]{3,4,2,1,0:T(8,128)(2,1)}, u32[]{:S(2)}) copy-start(bf16[3,3,3,64,32]{3,4,2,1,0:T(8,128)(2,1)} %param.4) | copy-start | bytes 331780
  1.6 0.7 %copy-start.1 = (bf16[64,1,128]{2,0,1:T(8,128)(2,1)S(1)}, bf16[64,1,128]{2,0,1:T(8,128)(2,1)}, u32[]{:S(2)}) copy-start(bf16[64,1,128]{2,0,1:T(8,128)(2,1)} %param.3) | copy-start | bytes 49156
  2.3 0.7 %copy-start.2 = (bf16[32,1,256]{2,0,1:T(8,128)(2,1)S(1)}, bf16[32,1,256]{2,0,1:T(8,128)(2,1)}, u32[]{:S(2)}) copy-start(bf16[32,1,256]{2,0,1:T(8,128)(2,1)} %param.5) | copy-start | bytes 49156

commit v2 on v0

v2 whole, which is shorter than its diff:
```python
import functools

import jax
import jax.numpy as jnp
from jax import lax
from jax.experimental import pallas as pl
from jax.experimental.pallas import tpu as pltpu
from jax.sharding import PartitionSpec as P

MESH = pl.DeviceIdType.MESH
BF16 = jnp.bfloat16
F32 = jnp.float32
B = 32
NX, NY = 4, 8
FAR = (4, 3, 5, 2, 6, 1, 7)
LANES = 128


def kernel(
    ns,
    act_hbm, w_hbm, og_hbm, resp_ref, grad_ref,
    a_ref, o_ref, w_ref, d_ref, g_ref, hd_ref, hg_ref, wr_ref, lf_ref, lb_ref, rg_ref, rd_ref,
    pb_ref, pf_ref, rb_ref, rf_ref,
    load_sem, f1_send, f1_recv, f2_send, f2_recv, b1_send, b1_recv, b2_send, b2_recv,
    ws_send, ws_recv, h_send, h_recv, b3_send, b3_recv, f3_send, f3_recv,
):
    chan, filt, s = lax.axis_index("chan"), lax.axis_index("filt"), lax.axis_index("sp")
    x, core = chan // 2, chan % 2
    zl, y = filt // NY, filt % NY
    k, xi = x // 2, x % 2
    other = 1 - core
    has_low, has_high = s > 0, s < ns - 1
    relay = core == k
    stays = core == zl

    def dev(x_, core_, zl_, y_, s_):
        return (x_ * 2 + core_, zl_ * NY + y_, s_)

    def remote(src, dst, ssem, rsem, to):
        return pltpu.make_async_remote_copy(
            src_ref=src, dst_ref=dst, send_sem=ssem, recv_sem=rsem,
            device_id=to, device_id_type=MESH,
        )

    def got(ref, sem):
        pltpu.make_async_copy(ref, ref, sem).wait()

    def start(args, own=None):
        if own is None:
            remote(*args).start()
            return
        pl.when(jnp.logical_not(own))(lambda: remote(*args).start())
        pl.when(own)(lambda: pltpu.make_async_copy(args[0], args[1], args[3]).start())

    def finish(args, own=None):
        if own is None:
            remote(*args).wait_send()
        else:
            pl.when(jnp.logical_not(own))(lambda: remote(*args).wait_send())

    barrier = pltpu.get_barrier_semaphore()

    def greet(to):
        pl.semaphore_signal(barrier, inc=1, device_id=to, device_id_type=MESH)

    loads = [
        pltpu.make_async_copy(act_hbm, a_ref.at[1], load_sem.at[0]),
        pltpu.make_async_copy(og_hbm, o_ref, load_sem.at[1]),
        pltpu.make_async_copy(w_hbm, w_ref, load_sem.at[2]),
    ]
    for load in loads:
        load.start()
    for d in FAR:
        for c in range(2):
            greet(dev(x, c, core, (y + d) % NY, s))

    def greet_slab(ds):
        for dc in range(2):
            for dz in range(2):
                if (ds, dc, dz) != (0, 0, 0):
                    greet(dev(x, (core + dc) % 2, (zl + dz) % 2, y, s + ds))

    pl.when(has_low)(lambda: greet_slab(-1))
    pl.when(has_high)(lambda: greet_slab(1))
    greet_slab(0)
    for d in range(1, NX):
        greet(dev((x + d) % NX, core, zl, y, s))

    def clear_planes(p):
        d_ref[:, p] = jnp.zeros((NY,) + d_ref.shape[2:], BF16)

        @pl.when(relay)
        def _():
            g_ref[xi, p] = jnp.zeros(g_ref.shape[2:], BF16)

    pl.when(jnp.logical_not(has_low))(lambda: clear_planes(0))
    pl.when(jnp.logical_not(has_high))(lambda: clear_planes(2))
    loads[0].wait()
    loads[1].wait()
    count = 2 * (NY - 1) + 3 + (NX - 1)
    pl.semaphore_wait(barrier, count + 4 * has_low.astype(jnp.int32) + 4 * has_high.astype(jnp.int32))

    def f1_copy(ds):
        return (a_ref.at[1], a_ref.at[1 - ds], f1_send.at[(ds + 1) // 2], f1_recv.at[(1 - ds) // 2],
                dev(x, core, zl, y, s + ds))

    def f2_sends(p):
        for d in (0,) + FAR:
            for dz in range(2):
                z2, y2 = (zl + dz) % 2, (y + d) % NY
                start((a_ref.at[p, pl.ds(z2 * B, B), :], d_ref.at[y, p, pl.ds(core * B, B), :],
                       f2_send.at[p], f2_recv.at[p], dev(x, zl, z2, y2, s)),
                      stays if (d, dz) == (0, 0) else None)

    def f2_finish(p):
        got(d_ref.at[pl.ds(0, NY - 1), p], f2_send.at[p])
        got(d_ref.at[NY - 1, p, pl.ds(0, B)], f2_send.at[p])
        pl.when(jnp.logical_not(stays))(lambda: got(d_ref.at[NY - 1, p, pl.ds(B, B)], f2_send.at[p]))

    def b1_copy(ds, dz):
        z2 = (zl + dz) % 2
        return (
            o_ref,
            g_ref.at[xi, 1 - ds, core, pl.ds(zl * B, B), :],
            b1_send.at[ds + 1, dz], b1_recv.at[1 - ds], dev(x, k, z2, y, s + ds),
        )

    def b1_sends(act):
        def slab(ds):
            for dz in range(2):
                act(b1_copy(ds, dz), relay if (ds, dz) == (0, 0) else None)

        pl.when(has_low)(lambda: slab(-1))
        pl.when(has_high)(lambda: slab(1))
        slab(0)

    pl.when(has_low)(lambda: start(f1_copy(-1)))
    pl.when(has_high)(lambda: start(f1_copy(1)))
    b1_sends(start)
    f2_sends(1)

    loads[2].wait()
    blank = jnp.zeros((B, B), BF16)
    for h in range(2):
        slot = jnp.where(zl == h, h, 2)
        for a in range(3):
            for e in range(3):
                taps = [w_ref[a * 9 + b * 3 + e] for b in range(3)]
                wr_ref[core, slot, 0, a * 3 + e] = jnp.concatenate(
                    [t[:, h * B:(h + 1) * B] for t in taps] + [blank], axis=1)
    w_across = (wr_ref.at[core, 2, 0], wr_ref.at[core, zl, 0], ws_send.at[0], ws_recv.at[0], dev(x, core, 1 - zl, y, s))
    w_own = (wr_ref.at[core, zl], wr_ref.at[core, zl], ws_send.at[1], ws_recv.at[1], dev(x, other, zl, y, s))
    w_next = (wr_ref.at[core, 1 - zl], wr_ref.at[core, 1 - zl], ws_send.at[2], ws_recv.at[2], dev(x, other, zl, y, s))
    start(w_across)

    def turn(slot):
        for i in range(9):
            flip = wr_ref[core, slot, 0, i].astype(F32).T
            wr_ref[core, slot, 1, i] = jnp.concatenate(
                [flip[(2 - b) * B:(3 - b) * B] for b in range(3)] + [flip[3 * B:]], axis=1).astype(BF16)

    def b2_copy(p, d):
        return (g_ref.at[xi, p], g_ref.at[xi, p], b2_send.at[p, d - 1], b2_recv.at[xi, p],
                dev((x + d) % NX, core, zl, y, s))

    def b2_sends(p):
        for d in (2, 1, 3):
            start(b2_copy(p, d))

    @pl.when(relay)
    def _():
        got(g_ref.at[xi, 1], b1_recv.at[1])
        b2_sends(1)

    @pl.when(has_low)
    def _():
        got(a_ref.at[0], f1_recv.at[0])
        f2_sends(0)

    @pl.when(has_high)
    def _():
        got(a_ref.at[2], f1_recv.at[1])
        f2_sends(2)

    @pl.when(relay)
    def _():
        pl.when(has_low)(lambda: got(g_ref.at[xi, 0], b1_recv.at[0]))
        b2_sends(0)
        pl.when(has_high)(lambda: got(g_ref.at[xi, 2], b1_recv.at[2]))
        b2_sends(2)

    turn(zl)
    start(w_own)
    got(wr_ref.at[core, 1 - zl, 0], ws_recv.at[0])
    turn(1 - zl)
    start(w_next)

    low_g = (g_ref.at[0, :, 0, :, pl.ds(0, LANES)], hg_ref, h_send.at[0], h_recv.at[0], dev(x, other, zl, y, s))
    high_g = (g_ref.at[1, :, 1, :, pl.ds(LANES, LANES)], hg_ref, h_send.at[0], h_recv.at[0], dev(x, other, zl, y, s))
    low_d = (d_ref.at[0], hd_ref, h_send.at[1], h_recv.at[1], dev(x, other, zl, y, s))
    high_d = (d_ref.at[NY - 1], hd_ref, h_send.at[1], h_recv.at[1], dev(x, other, zl, y, s))

    for i in range(2):
        @pl.when(jnp.logical_not(jnp.logical_and(relay, xi == i)))
        def _(i=i):
            for p in range(3):
                got(g_ref.at[i, p], b2_recv.at[i, p])

    pl.when(core == 0)(lambda: start(high_g))
    pl.when(core == 1)(lambda: start(low_g))

    remote(*w_own).wait_recv()
    remote(*w_next).wait_recv()
    for cs in range(2):
        for z in range(2):
            for a in range(3):
                for e in range(3):
                    lf_ref[e * 64 + z * B:e * 64 + z * B + B, a * 256 + cs * 128:a * 256 + cs * 128 + 128] = (
                        wr_ref[cs, z, 0, a * 3 + e])
                    lb_ref[e * 64 + cs * B:e * 64 + cs * B + B, a * 256 + z * 128:a * 256 + z * 128 + 128] = (
                        wr_ref[cs, z, 1, (2 - a) * 3 + 2 - e])

    lane = lax.broadcasted_iota(jnp.int32, (64, LANES), 1)
    left_half = lane < 64
    inside_low = lane % 64 != 0
    inside_high = lane % 64 != 63

    def put(r_ref, a, b, t, tile):
        for c in range(2):
            row = a * 256 + c * 128 + b * B
            r_ref[row:row + B, t * LANES:(t + 1) * LANES] = tile[c * B:(c + 1) * B]

    def half_turn(tile):
        return pltpu.roll(tile.astype(F32), 64, axis=1)

    def rows(r_ref, a, tile_of):
        for c in range(2):
            row = a * 256 + c * 128 + 3 * B
            r_ref[row:row + B, :] = jnp.zeros((B, r_ref.shape[1]), BF16)
        turned = None
        for t in range(NY):
            tile = tile_of(a, t)
            put(r_ref, a, 1, t, tile)
            before, turned = turned, half_turn(tile)
            if t > 0:
                mid = jnp.where(left_half, before, turned).astype(BF16)
                put(r_ref, a, 0, t, mid)
                put(r_ref, a, 2, t - 1, mid)

    def edge_rows(r_ref, a, tile_of, halo):
        turned = half_turn(halo)
        none = jnp.zeros_like(turned)
        low = jnp.where(core == 1, turned, none)
        high = jnp.where(core == 0, turned, none)
        put(r_ref, a, 0, 0, jnp.where(left_half, low, half_turn(tile_of(a, 0))).astype(BF16))
        put(r_ref, a, 2, NY - 1, jnp.where(left_half, half_turn(tile_of(a, NY - 1)), high).astype(BF16))

    def multiply(l_ref, r_ref, pair, emit):
        part = jnp.dot(l_ref[...], r_ref[:, pair * 256:(pair + 1) * 256], preferred_element_type=F32)
        for h in range(2):
            piece = part[:, h * LANES:(h + 1) * LANES]
            total = piece[64:128]
            total += jnp.where(inside_low, pltpu.roll(piece[0:64], 1, axis=1), 0.0)
            total += jnp.where(inside_high, pltpu.roll(piece[128:192], LANES - 1, axis=1), 0.0)
            emit(pair * 2 + h, total)

    def g_tile(a, t):
        return g_ref[t // 4, a, t // 2 % 2, :, t % 2 * LANES:(t % 2 + 1) * LANES]

    def emit_b(t, total):
        pb_ref[t] = total

    for a in range(3):
        rows(rg_ref, a, g_tile)
    for pair in (1, 2):
        multiply(lb_ref, rg_ref, pair, emit_b)
    pl.when(core == 0)(lambda: remote(*low_g).wait_recv())
    pl.when(core == 1)(lambda: remote(*high_g).wait_recv())
    for a in range(3):
        edge_rows(rg_ref, a, g_tile, hg_ref[a])
    for pair in (0, 3):
        multiply(lb_ref, rg_ref, pair, emit_b)

    got(d_ref.at[:, 1], f2_recv.at[1])
    for d in (0,) + FAR:
        for dc in range(2):
            y2, c2 = (y + d) % NY, (core + dc) % 2
            start((pb_ref.at[y2, pl.ds(c2 * B, B), :], rb_ref.at[y, pl.ds(zl * B, B), :],
                   b3_send, b3_recv, dev(x, c2, core, y2, s)),
                  stays if (d, dc) == (0, 0) else None)

    def d_tile(a, t):
        return d_ref[t, a]

    rows(rd_ref, 1, d_tile)
    pl.when(has_low)(lambda: got(d_ref.at[:, 0], f2_recv.at[0]))
    pl.when(has_high)(lambda: got(d_ref.at[:, 2], f2_recv.at[2]))
    pl.when(core == 0)(lambda: start(high_d))
    pl.when(core == 1)(lambda: start(low_d))
    rows(rd_ref, 0, d_tile)
    rows(rd_ref, 2, d_tile)

    def emit_f(t, total):
        for z in range(2):
            pf_ref[t // 2, z, :, t % 2 * LANES:(t % 2 + 1) * LANES] = total[z * B:(z + 1) * B]

    def f3_sends(j):
        for dz in range(2):
            x2, c2, z2 = core * 2 + j // 2, j % 2, (zl + dz) % 2
            own = jnp.logical_and(x2 == x, c2 == core) if dz == 0 else None
            start((pf_ref.at[j, z2], rf_ref.at[x, zl], f3_send.at[j, dz], f3_recv, dev(x2, c2, z2, y, s)), own)

    def f3_finish(j):
        for dz in range(2):
            x2, c2, z2 = core * 2 + j // 2, j % 2, (zl + dz) % 2
            own = jnp.logical_and(x2 == x, c2 == core) if dz == 0 else None
            finish((pf_ref.at[j, z2], rf_ref.at[x, zl], f3_send.at[j, dz], f3_recv, dev(x2, c2, z2, y, s)), own)

    for pair in (1, 2):
        multiply(lf_ref, rd_ref, pair, emit_f)
        f3_sends(pair)
    pl.when(core == 0)(lambda: remote(*low_d).wait_recv())
    pl.when(core == 1)(lambda: remote(*high_d).wait_recv())
    for a in range(3):
        edge_rows(rd_ref, a, d_tile, hd_ref[a])
    for pair in (0, 3):
        multiply(lf_ref, rd_ref, pair, emit_f)
        f3_sends(pair)

    got(rb_ref, b3_recv)
    total = rb_ref[0]
    for i in range(1, NY):
        total += rb_ref[i]
    grad_ref[...] = total.astype(BF16)

    pl.when(has_low)(lambda: finish(f1_copy(-1)))
    pl.when(has_high)(lambda: finish(f1_copy(1)))
    b1_sends(finish)
    f2_finish(1)
    pl.when(has_low)(lambda: f2_finish(0))
    pl.when(has_high)(lambda: f2_finish(2))
    for copy in (w_across, w_own, w_next):
        finish(copy)

    @pl.when(relay)
    def _():
        for p in range(3):
            for d in range(1, NX):
                finish(b2_copy(p, d))

    pl.when(core == 0)(lambda: finish(high_g))
    pl.when(core == 1)(lambda: finish(low_g))
    pl.when(core == 0)(lambda: finish(high_d))
    pl.when(core == 1)(lambda: finish(low_d))
    got(pb_ref.at[pl.ds(0, NY - 1)], b3_send)
    got(pb_ref.at[NY - 1, pl.ds(0, B)], b3_send)
    pl.when(jnp.logical_not(stays))(lambda: got(pb_ref.at[NY - 1, pl.ds(B, B)], b3_send))
    for j in range(NX):
        f3_finish(j)

    got(rf_ref, f3_recv)
    total = rf_ref[0, 0]
    for i in range(1, NX * 2):
        total += rf_ref[i // 2, i % 2]
    resp_ref[...] = total.astype(BF16)


def solution(mesh):
    ns = mesh.shape["sp"]

    def local(activations, weights, out_grad):
        act = activations.reshape(2 * B, LANES)
        grad = out_grad.reshape(B, -1)
        wide = grad.shape[1]
        w = jnp.swapaxes(weights, 3, 4).reshape(27, B, 2 * B)
        dma = pltpu.SemaphoreType.DMA
        responses, in_grad = pl.pallas_call(
            functools.partial(kernel, ns),
            out_shape=(
                jax.ShapeDtypeStruct((B, wide), BF16),
                jax.ShapeDtypeStruct((2 * B, LANES), BF16),
            ),
            in_specs=[pl.BlockSpec(memory_space=pl.ANY)] * 3,
            out_specs=(pl.BlockSpec(memory_space=pltpu.VMEM),) * 2,
            scratch_shapes=[
                pltpu.VMEM((3, 2 * B, LANES), BF16),
                pltpu.VMEM((B, wide), BF16),
                pltpu.VMEM((27, B, 2 * B), BF16),
                pltpu.VMEM((NY, 3, 2 * B, LANES), BF16),
                pltpu.VMEM((2, 3, 2, 2 * B, wide), BF16),
                pltpu.VMEM((3, 2 * B, LANES), BF16),
                pltpu.VMEM((3, 2 * B, LANES), BF16),
                pltpu.VMEM((2, 3, 2, 9, B, LANES), BF16),
                pltpu.VMEM((192, 768), BF16),
                pltpu.VMEM((192, 768), BF16),
                pltpu.VMEM((768, NY * LANES), BF16),
                pltpu.VMEM((768, NY * LANES), BF16),
                pltpu.VMEM((NY, 2 * B, LANES), F32),
                pltpu.VMEM((NX, 2, B, wide), F32),
                pltpu.VMEM((NY, 2 * B, LANES), F32),
                pltpu.VMEM((NX, 2, B, wide), F32),
                dma((3,)),
                dma((2,)), dma((2,)),
                dma((3,)), dma((3,)),
                dma((3, 2)), dma((3,)),
                dma((3, NX - 1)), dma((2, 3)),
                dma((3,)), dma((3,)),
                dma((2,)), dma((2,)),
                dma, dma,
                dma((NX, 2)), dma,
            ],
            compiler_params=pltpu.CompilerParams(
                collective_id=0, has_side_effects=True, vmem_limit_bytes=60 * 1024 * 1024,
            ),
        )(act, w, grad)
        return responses.reshape(out_grad.shape), in_grad.reshape(activations.shape)

    return jax.shard_map(
        local,
        mesh=mesh,
        in_specs=(
            P("chan", "sp", "filt"),
            P(None, None, None, "chan", "filt"),
            P("filt", "sp", "chan"),
        ),
        out_specs=(P("filt", "sp", "chan"), P("chan", "sp", "filt")),
        check_vma=False,
    )
```

time: 388 us -> 36.7 us (0.09)
  the two profiles are of different devices: /device:TPU:4 before, /device:TPU:1 now
where the time goes in v2:
time: 36.7 us; the launch traced here: 36.5 us
  Pallas kernels  33.9 us (92%)
  local copies, waits for them, and re-layouts  1.94 us (5%)
  between operations  0.65 us (2%)
    pallas_call x1, Pallas kernels, local(): pl.pallas_call(functools.partial(kernel, ns), out_shape=(jax.ShapeDtypeSt...  33.9 us
    unnamed x4, local copies, waits for them, and re-layouts  1.94 us

profile of v2, /device:TPU:1, one launch (start us, length us, event | category | flops | bytes accessed | tf_op | source)
XLA Modules:
  0.0 36.5 jit_solution(8658997308138425787)
XLA Ops:
  0.6 33.9 %shard_map.50 = (bf16[32,256]{1,0:T(8,128)(2,1)}, bf16[64,128]{1,0:T(8,128)(2,1)}) custom-call(bf16[64,128]{1,0:T(8,128)(2,1)} %bitcast.8, bf16[27,32,64]{2,1,0:T(8,128)(2,1)} %bitcast.7, bf16[32,256]{1,0:T(8,128)(2,1)} %bitcast.9), custom_call_target="tpu_custom_call" | custom-call | tf_op jit(solution)/shard_map/pallas_call | solution.py:377
  34.5 0.0 copy-start
  34.5 1.3 %copy.7 = bf16[32,1,256]{2,0,1:T(8,128)(2,1)} copy(bf16[32,1,256]{2,0,1:T(8,128)(2,1)} %bitcast.11) | data formatting | bytes 32768
  35.9 0.0 copy-done
  35.9 0.6 %copy.8 = bf16[64,1,128]{2,0,1:T(8,128)(2,1)} copy(bf16[64,1,128]{2,0,1:T(8,128)(2,1)S(1)} %bitcast.10) | data formatting | bytes 32768
Async XLA Ops:
  34.5 1.3 %copy-start = (bf16[64,128]{1,0:T(8,128)(2,1)S(1)}, bf16[64,128]{1,0:T(8,128)(2,1)}, u32[]{:S(2)}) copy-start(bf16[64,128]{1,0:T(8,128)(2,1)} %get-tuple-element.5) | copy-start | bytes 49156

commit v3 on v2

--- a/solution.py
+++ b/solution.py
@@ -104,9 +104,9 @@
         return (a_ref.at[1], a_ref.at[1 - ds], f1_send.at[(ds + 1) // 2], f1_recv.at[(1 - ds) // 2],
                 dev(x, core, zl, y, s + ds))
 
-    def f2_sends(p):
+    def f2_sends(p, across):
         for d in (0,) + FAR:
-            for dz in range(2):
+            for dz in across:
                 z2, y2 = (zl + dz) % 2, (y + d) % NY
                 start((a_ref.at[p, pl.ds(z2 * B, B), :], d_ref.at[y, p, pl.ds(core * B, B), :],
                        f2_send.at[p], f2_recv.at[p], dev(x, zl, z2, y2, s)),
@@ -122,22 +122,19 @@
         return (
             o_ref,
             g_ref.at[xi, 1 - ds, core, pl.ds(zl * B, B), :],
-            b1_send.at[ds + 1, dz], b1_recv.at[1 - ds], dev(x, k, z2, y, s + ds),
+            b1_send.at[ds + 1], b1_recv.at[1 - ds], dev(x, k, z2, y, s + ds),
         )
 
-    def b1_sends(act):
-        def slab(ds):
-            for dz in range(2):
-                act(b1_copy(ds, dz), relay if (ds, dz) == (0, 0) else None)
-
-        pl.when(has_low)(lambda: slab(-1))
-        pl.when(has_high)(lambda: slab(1))
-        slab(0)
+    def b1_sends(ds):
+        for dz in range(2):
+            start(b1_copy(ds, dz), relay if (ds, dz) == (0, 0) else None)
 
     pl.when(has_low)(lambda: start(f1_copy(-1)))
     pl.when(has_high)(lambda: start(f1_copy(1)))
-    b1_sends(start)
-    f2_sends(1)
+    pl.when(has_low)(lambda: b1_sends(-1))
+    pl.when(has_high)(lambda: b1_sends(1))
+    b1_sends(0)
+    f2_sends(1, (0,))
 
     loads[2].wait()
     blank = jnp.zeros((B, B), BF16)
@@ -160,7 +157,7 @@
                 [flip[(2 - b) * B:(3 - b) * B] for b in range(3)] + [flip[3 * B:]], axis=1).astype(BF16)
 
     def b2_copy(p, d):
-        return (g_ref.at[xi, p], g_ref.at[xi, p], b2_send.at[p, d - 1], b2_recv.at[xi, p],
+        return (g_ref.at[xi, p], g_ref.at[xi, p], b2_send.at[p], b2_recv.at[xi, p],
                 dev((x + d) % NX, core, zl, y, s))
 
     def b2_sends(p):
@@ -172,15 +169,17 @@
         got(g_ref.at[xi, 1], b1_recv.at[1])
         b2_sends(1)
 
+    f2_sends(1, (1,))
+
     @pl.when(has_low)
     def _():
         got(a_ref.at[0], f1_recv.at[0])
-        f2_sends(0)
+        f2_sends(0, (0, 1))
 
     @pl.when(has_high)
     def _():
         got(a_ref.at[2], f1_recv.at[1])
-        f2_sends(2)
+        f2_sends(2, (0, 1))
 
     @pl.when(relay)
     def _():
@@ -270,24 +269,27 @@
     def emit_b(t, total):
         pb_ref[t] = total
 
+    def b3_sends(tiles):
+        for t in tiles:
+            for dc in range(2):
+                c2 = (core + dc) % 2
+                start((pb_ref.at[t, pl.ds(c2 * B, B), :], rb_ref.at[y, pl.ds(zl * B, B), :],
+                       b3_send, b3_recv, dev(x, c2, core, t, s)),
+                      jnp.logical_and(stays, y == t) if dc == 0 else None)
+
     for a in range(3):
         rows(rg_ref, a, g_tile)
     for pair in (1, 2):
         multiply(lb_ref, rg_ref, pair, emit_b)
+    got(d_ref.at[:, 1], f2_recv.at[1])
+    b3_sends((4, 3, 5, 2))
     pl.when(core == 0)(lambda: remote(*low_g).wait_recv())
     pl.when(core == 1)(lambda: remote(*high_g).wait_recv())
     for a in range(3):
         edge_rows(rg_ref, a, g_tile, hg_ref[a])
     for pair in (0, 3):
         multiply(lb_ref, rg_ref, pair, emit_b)
-
-    got(d_ref.at[:, 1], f2_recv.at[1])
-    for d in (0,) + FAR:
-        for dc in range(2):
-            y2, c2 = (y + d) % NY, (core + dc) % 2
-            start((pb_ref.at[y2, pl.ds(c2 * B, B), :], rb_ref.at[y, pl.ds(zl * B, B), :],
-                   b3_send, b3_recv, dev(x, c2, core, y2, s)),
-                  stays if (d, dc) == (0, 0) else None)
+    b3_sends((0, 7, 1, 6))
 
     def d_tile(a, t):
         return d_ref[t, a]
@@ -308,13 +310,7 @@
         for dz in range(2):
             x2, c2, z2 = core * 2 + j // 2, j % 2, (zl + dz) % 2
             own = jnp.logical_and(x2 == x, c2 == core) if dz == 0 else None
-            start((pf_ref.at[j, z2], rf_ref.at[x, zl], f3_send.at[j, dz], f3_recv, dev(x2, c2, z2, y, s)), own)
-
-    def f3_finish(j):
-        for dz in range(2):
-            x2, c2, z2 = core * 2 + j // 2, j % 2, (zl + dz) % 2
-            own = jnp.logical_and(x2 == x, c2 == core) if dz == 0 else None
-            finish((pf_ref.at[j, z2], rf_ref.at[x, zl], f3_send.at[j, dz], f3_recv, dev(x2, c2, z2, y, s)), own)
+            start((pf_ref.at[j, z2], rf_ref.at[x, zl], f3_send, f3_recv, dev(x2, c2, z2, y, s)), own)
 
     for pair in (1, 2):
         multiply(lf_ref, rd_ref, pair, emit_f)
@@ -327,15 +323,13 @@
         multiply(lf_ref, rd_ref, pair, emit_f)
         f3_sends(pair)
 
-    got(rb_ref, b3_recv)
-    total = rb_ref[0]
-    for i in range(1, NY):
-        total += rb_ref[i]
-    grad_ref[...] = total.astype(BF16)
-
     pl.when(has_low)(lambda: finish(f1_copy(-1)))
     pl.when(has_high)(lambda: finish(f1_copy(1)))
-    b1_sends(finish)
+    pair = g_ref.at[0, 0, 0]
+    pl.when(has_low)(lambda: got(pair, b1_send.at[0]))
+    pl.when(has_high)(lambda: got(pair, b1_send.at[2]))
+    pl.when(relay)(lambda: got(pair.at[pl.ds(0, B)], b1_send.at[1]))
+    pl.when(jnp.logical_not(relay))(lambda: got(pair, b1_send.at[1]))
     f2_finish(1)
     pl.when(has_low)(lambda: f2_finish(0))
     pl.when(has_high)(lambda: f2_finish(2))
@@ -345,8 +339,7 @@
     @pl.when(relay)
     def _():
         for p in range(3):
-            for d in range(1, NX):
-                finish(b2_copy(p, d))
+            got(g_ref.at[0], b2_send.at[p])
 
     pl.when(core == 0)(lambda: finish(high_g))
     pl.when(core == 1)(lambda: finish(low_g))
@@ -355,14 +348,21 @@
     got(pb_ref.at[pl.ds(0, NY - 1)], b3_send)
     got(pb_ref.at[NY - 1, pl.ds(0, B)], b3_send)
     pl.when(jnp.logical_not(stays))(lambda: got(pb_ref.at[NY - 1, pl.ds(B, B)], b3_send))
-    for j in range(NX):
-        f3_finish(j)
+    got(pf_ref.at[pl.ds(0, NX - 1)], f3_send)
+    got(pf_ref.at[NX - 1, 0], f3_send)
+    pl.when(jnp.logical_not(relay))(lambda: got(pf_ref.at[NX - 1, 1], f3_send))
 
     got(rf_ref, f3_recv)
     total = rf_ref[0, 0]
     for i in range(1, NX * 2):
         total += rf_ref[i // 2, i % 2]
     resp_ref[...] = total.astype(BF16)
+
+    got(rb_ref, b3_recv)
+    total = rb_ref[0]
+    for i in range(1, NY):
+        total += rb_ref[i]
+    grad_ref[...] = total.astype(BF16)
 
 
 def solution(mesh):
@@ -377,8 +377,8 @@
         responses, in_grad = pl.pallas_call(
             functools.partial(kernel, ns),
             out_shape=(
-                jax.ShapeDtypeStruct((B, wide), BF16),
-                jax.ShapeDtypeStruct((2 * B, LANES), BF16),
+                pltpu.VMEM((B, wide), BF16),
+                pltpu.VMEM((2 * B, LANES), BF16),
             ),
             in_specs=[pl.BlockSpec(memory_space=pl.ANY)] * 3,
             out_specs=(pl.BlockSpec(memory_space=pltpu.VMEM),) * 2,
@@ -402,12 +402,12 @@
                 dma((3,)),
                 dma((2,)), dma((2,)),
                 dma((3,)), dma((3,)),
-                dma((3, 2)), dma((3,)),
-                dma((3, NX - 1)), dma((2, 3)),
+                dma((3,)), dma((3,)),
+                dma((3,)), dma((2, 3)),
                 dma((3,)), dma((3,)),
                 dma((2,)), dma((2,)),
                 dma, dma,
-                dma((NX, 2)), dma,
+                dma, dma,
             ],
             compiler_params=pltpu.CompilerParams(
                 collective_id=0, has_side_effects=True, vmem_limit_bytes=60 * 1024 * 1024,

time: 36.7 us -> 34.5 us (0.940)
  the two profiles are of different devices: /device:TPU:1 before, /device:TPU:137 now
where the time goes in v3:
time: 34.5 us; the launch traced here: 34.3 us
  Pallas kernels  32.4 us (94%)
  local copies, waits for them, and re-layouts  1.21 us (4%)
  between operations  0.64 us (2%)
    pallas_call x1, Pallas kernels, local(): pl.pallas_call(functools.partial(kernel, ns), out_shape=(pltpu.VMEM((B, w...  32.4 us
    unnamed x2, local copies, waits for them, and re-layouts  1.21 us

profile of v3, /device:TPU:137, one launch (start us, length us, event | category | flops | bytes accessed | tf_op | source)
XLA Modules:
  0.0 34.3 jit_solution(11493958195546350304)
XLA Ops:
  0.6 32.4 %shard_map.50 = (bf16[32,256]{1,0:T(8,128)(2,1)S(1)}, bf16[64,128]{1,0:T(8,128)(2,1)S(1)}) custom-call(bf16[64,128]{1,0:T(8,128)(2,1)} %bitcast.10, bf16[27,32,64]{2,1,0:T(8,128)(2,1)} %bitcast.9, bf16[32,256]{1,0:T(8,128)(2,1)} %bitcast.11), custom_call_target="tpu_custom_call" | custom-call | tf_op jit(solution)/shard_map/pallas_call | solution.py:377
  33.1 0.6 %copy.7 = bf16[32,1,256]{2,0,1:T(8,128)(2,1)} copy(bf16[32,1,256]{2,0,1:T(8,128)(2,1)S(1)} %bitcast.8) | data formatting | bytes 32768
  33.7 0.6 %copy.8 = bf16[64,1,128]{2,0,1:T(8,128)(2,1)} copy(bf16[64,1,128]{2,0,1:T(8,128)(2,1)S(1)} %bitcast.7) | data formatting | bytes 32768

commit v4 on v3

--- a/solution.py
+++ b/solution.py
@@ -22,7 +22,7 @@
     a_ref, o_ref, w_ref, d_ref, g_ref, hd_ref, hg_ref, wr_ref, lf_ref, lb_ref, rg_ref, rd_ref,
     pb_ref, pf_ref, rb_ref, rf_ref,
     load_sem, f1_send, f1_recv, f2_send, f2_recv, b1_send, b1_recv, b2_send, b2_recv,
-    ws_send, ws_recv, h_send, h_recv, b3_send, b3_recv, f3_send, f3_recv,
+    ws_send, ws_recv, h_send, h_recv, b3_send, b3_recv, f3_send, f3_recv, up_sem,
 ):
     chan, filt, s = lax.axis_index("chan"), lax.axis_index("filt"), lax.axis_index("sp")
     x, core = chan // 2, chan % 2
@@ -60,8 +60,8 @@
 
     barrier = pltpu.get_barrier_semaphore()
 
-    def greet(to):
-        pl.semaphore_signal(barrier, inc=1, device_id=to, device_id_type=MESH)
+    def greet(to, sem=barrier):
+        pl.semaphore_signal(sem, inc=1, device_id=to, device_id_type=MESH)
 
     loads = [
         pltpu.make_async_copy(act_hbm, a_ref.at[1], load_sem.at[0]),
@@ -80,7 +80,6 @@
                 if (ds, dc, dz) != (0, 0, 0):
                     greet(dev(x, (core + dc) % 2, (zl + dz) % 2, y, s + ds))
 
-    pl.when(has_low)(lambda: greet_slab(-1))
     pl.when(has_high)(lambda: greet_slab(1))
     greet_slab(0)
     for d in range(1, NX):
@@ -98,7 +97,13 @@
     loads[0].wait()
     loads[1].wait()
     count = 2 * (NY - 1) + 3 + (NX - 1)
-    pl.semaphore_wait(barrier, count + 4 * has_low.astype(jnp.int32) + 4 * has_high.astype(jnp.int32))
+    pl.semaphore_wait(barrier, count + 4 * has_low.astype(jnp.int32))
+
+    @pl.when(has_low)
+    def _():
+        for dc in range(2):
+            for dz in range(2):
+                greet(dev(x, (core + dc) % 2, (zl + dz) % 2, y, s - 1), up_sem)
 
     def f1_copy(ds):
         return (a_ref.at[1], a_ref.at[1 - ds], f1_send.at[(ds + 1) // 2], f1_recv.at[(1 - ds) // 2],
@@ -130,11 +135,9 @@
             start(b1_copy(ds, dz), relay if (ds, dz) == (0, 0) else None)
 
     pl.when(has_low)(lambda: start(f1_copy(-1)))
-    pl.when(has_high)(lambda: start(f1_copy(1)))
     pl.when(has_low)(lambda: b1_sends(-1))
-    pl.when(has_high)(lambda: b1_sends(1))
     b1_sends(0)
-    f2_sends(1, (0,))
+    f2_sends(1, (0, 1))
 
     loads[2].wait()
     blank = jnp.zeros((B, B), BF16)
@@ -156,6 +159,12 @@
             wr_ref[core, slot, 1, i] = jnp.concatenate(
                 [flip[(2 - b) * B:(3 - b) * B] for b in range(3)] + [flip[3 * B:]], axis=1).astype(BF16)
 
+    @pl.when(has_high)
+    def _():
+        pl.semaphore_wait(up_sem, 4)
+        start(f1_copy(1))
+        b1_sends(1)
+
     def b2_copy(p, d):
         return (g_ref.at[xi, p], g_ref.at[xi, p], b2_send.at[p], b2_recv.at[xi, p],
                 dev((x + d) % NX, core, zl, y, s))
@@ -168,8 +177,6 @@
     def _():
         got(g_ref.at[xi, 1], b1_recv.at[1])
         b2_sends(1)
-
-    f2_sends(1, (1,))
 
     @pl.when(has_low)
     def _():
@@ -194,19 +201,14 @@
     turn(1 - zl)
     start(w_next)
 
-    low_g = (g_ref.at[0, :, 0, :, pl.ds(0, LANES)], hg_ref, h_send.at[0], h_recv.at[0], dev(x, other, zl, y, s))
-    high_g = (g_ref.at[1, :, 1, :, pl.ds(LANES, LANES)], hg_ref, h_send.at[0], h_recv.at[0], dev(x, other, zl, y, s))
-    low_d = (d_ref.at[0], hd_ref, h_send.at[1], h_recv.at[1], dev(x, other, zl, y, s))
-    high_d = (d_ref.at[NY - 1], hd_ref, h_send.at[1], h_recv.at[1], dev(x, other, zl, y, s))
-
-    for i in range(2):
-        @pl.when(jnp.logical_not(jnp.logical_and(relay, xi == i)))
-        def _(i=i):
-            for p in range(3):
-                got(g_ref.at[i, p], b2_recv.at[i, p])
-
-    pl.when(core == 0)(lambda: start(high_g))
-    pl.when(core == 1)(lambda: start(low_g))
+    def low_g(p):
+        return (g_ref.at[0, p, 0, :, pl.ds(0, LANES)], hg_ref.at[p], h_send.at[p], h_recv.at[p], dev(x, other, zl, y, s))
+
+    def high_g(p):
+        return (g_ref.at[1, p, 1, :, pl.ds(LANES, LANES)], hg_ref.at[p], h_send.at[p], h_recv.at[p], dev(x, other, zl, y, s))
+
+    low_d = (d_ref.at[0], hd_ref, h_send.at[3], h_recv.at[3], dev(x, other, zl, y, s))
+    high_d = (d_ref.at[NY - 1], hd_ref, h_send.at[3], h_recv.at[3], dev(x, other, zl, y, s))
 
     remote(*w_own).wait_recv()
     remote(*w_next).wait_recv()
@@ -277,16 +279,22 @@
                        b3_send, b3_recv, dev(x, c2, core, t, s)),
                       jnp.logical_and(stays, y == t) if dc == 0 else None)
 
-    for a in range(3):
-        rows(rg_ref, a, g_tile)
+    for p in (1, 0, 2):
+        for i in range(2):
+            @pl.when(jnp.logical_not(jnp.logical_and(relay, xi == i)))
+            def _(i=i, p=p):
+                got(g_ref.at[i, p], b2_recv.at[i, p])
+
+        pl.when(core == 0)(lambda: start(high_g(p)))
+        pl.when(core == 1)(lambda: start(low_g(p)))
+        rows(rg_ref, p, g_tile)
     for pair in (1, 2):
         multiply(lb_ref, rg_ref, pair, emit_b)
     got(d_ref.at[:, 1], f2_recv.at[1])
     b3_sends((4, 3, 5, 2))
-    pl.when(core == 0)(lambda: remote(*low_g).wait_recv())
-    pl.when(core == 1)(lambda: remote(*high_g).wait_recv())
-    for a in range(3):
-        edge_rows(rg_ref, a, g_tile, hg_ref[a])
+    for p in range(3):
+        got(hg_ref.at[p], h_recv.at[p])
+        edge_rows(rg_ref, p, g_tile, hg_ref[p])
     for pair in (0, 3):
         multiply(lb_ref, rg_ref, pair, emit_b)
     b3_sends((0, 7, 1, 6))
@@ -341,8 +349,8 @@
         for p in range(3):
             got(g_ref.at[0], b2_send.at[p])
 
-    pl.when(core == 0)(lambda: finish(high_g))
-    pl.when(core == 1)(lambda: finish(low_g))
+    for p in range(3):
+        got(hg_ref.at[p], h_send.at[p])
     pl.when(core == 0)(lambda: finish(high_d))
     pl.when(core == 1)(lambda: finish(low_d))
     got(pb_ref.at[pl.ds(0, NY - 1)], b3_send)
@@ -405,9 +413,10 @@
                 dma((3,)), dma((3,)),
                 dma((3,)), dma((2, 3)),
                 dma((3,)), dma((3,)),
-                dma((2,)), dma((2,)),
+                dma((4,)), dma((4,)),
                 dma, dma,
                 dma, dma,
+                pltpu.SemaphoreType.REGULAR,
             ],
             compiler_params=pltpu.CompilerParams(
                 collective_id=0, has_side_effects=True, vmem_limit_bytes=60 * 1024 * 1024,

time: 34.5 us -> 33.7 us (0.977)
  the two profiles are of different devices: /device:TPU:137 before, /device:TPU:384 now
where the time goes in v4:
time: 33.7 us; the launch traced here: 33.5 us
  Pallas kernels  31.6 us (94%)
  local copies, waits for them, and re-layouts  1.21 us (4%)
  between operations  0.64 us (2%)
    pallas_call x1, Pallas kernels, local(): pl.pallas_call(functools.partial(kernel, ns), out_shape=(pltpu.VMEM((B, w...  31.6 us
    unnamed x2, local copies, waits for them, and re-layouts  1.21 us

profile of v4, /device:TPU:384, one launch (start us, length us, event | category | flops | bytes accessed | tf_op | source)
XLA Modules:
  0.0 33.5 jit_solution(10378159554992380929)
XLA Ops:
  0.6 31.6 %shard_map.50 = (bf16[32,256]{1,0:T(8,128)(2,1)S(1)}, bf16[64,128]{1,0:T(8,128)(2,1)S(1)}) custom-call(bf16[64,128]{1,0:T(8,128)(2,1)} %bitcast.10, bf16[27,32,64]{2,1,0:T(8,128)(2,1)} %bitcast.9, bf16[32,256]{1,0:T(8,128)(2,1)} %bitcast.11), custom_call_target="tpu_custom_call" | custom-call | tf_op jit(solution)/shard_map/pallas_call | solution.py:385
  32.3 0.6 %copy.7 = bf16[32,1,256]{2,0,1:T(8,128)(2,1)} copy(bf16[32,1,256]{2,0,1:T(8,128)(2,1)S(1)} %bitcast.8) | data formatting | bytes 32768
  32.9 0.6 %copy.8 = bf16[64,1,128]{2,0,1:T(8,128)(2,1)} copy(bf16[64,1,128]{2,0,1:T(8,128)(2,1)S(1)} %bitcast.7) | data formatting | bytes 32768

commit v5 on v4

--- a/solution.py
+++ b/solution.py
@@ -21,8 +21,7 @@
     act_hbm, w_hbm, og_hbm, resp_ref, grad_ref,
     a_ref, o_ref, w_ref, d_ref, g_ref, hd_ref, hg_ref, wr_ref, lf_ref, lb_ref, rg_ref, rd_ref,
     pb_ref, pf_ref, rb_ref, rf_ref,
-    load_sem, f1_send, f1_recv, f2_send, f2_recv, b1_send, b1_recv, b2_send, b2_recv,
-    ws_send, ws_recv, h_send, h_recv, b3_send, b3_recv, f3_send, f3_recv, up_sem,
+    load_sem, sent, f1_recv, f2_recv, b1_recv, b2_recv, ws_recv, h_recv, b3_recv, f3_recv, up_sem,
 ):
     chan, filt, s = lax.axis_index("chan"), lax.axis_index("filt"), lax.axis_index("sp")
     x, core = chan // 2, chan % 2
@@ -106,28 +105,28 @@
                 greet(dev(x, (core + dc) % 2, (zl + dz) % 2, y, s - 1), up_sem)
 
     def f1_copy(ds):
-        return (a_ref.at[1], a_ref.at[1 - ds], f1_send.at[(ds + 1) // 2], f1_recv.at[(1 - ds) // 2],
+        return (a_ref.at[1], a_ref.at[1 - ds], sent, f1_recv.at[(1 - ds) // 2],
                 dev(x, core, zl, y, s + ds))
 
     def f2_sends(p, across):
-        for d in (0,) + FAR:
+        for y2 in (0, 1, 7, 2, 6, 3, 5, 4):
             for dz in across:
-                z2, y2 = (zl + dz) % 2, (y + d) % NY
+                z2 = (zl + dz) % 2
                 start((a_ref.at[p, pl.ds(z2 * B, B), :], d_ref.at[y, p, pl.ds(core * B, B), :],
-                       f2_send.at[p], f2_recv.at[p], dev(x, zl, z2, y2, s)),
-                      stays if (d, dz) == (0, 0) else None)
+                       sent, f2_recv.at[p], dev(x, zl, z2, y2, s)),
+                      jnp.logical_and(stays, y == y2) if dz == 0 else None)
 
     def f2_finish(p):
-        got(d_ref.at[pl.ds(0, NY - 1), p], f2_send.at[p])
-        got(d_ref.at[NY - 1, p, pl.ds(0, B)], f2_send.at[p])
-        pl.when(jnp.logical_not(stays))(lambda: got(d_ref.at[NY - 1, p, pl.ds(B, B)], f2_send.at[p]))
+        got(d_ref.at[pl.ds(0, NY - 1), p], sent)
+        got(d_ref.at[NY - 1, p, pl.ds(0, B)], sent)
+        pl.when(jnp.logical_not(stays))(lambda: got(d_ref.at[NY - 1, p, pl.ds(B, B)], sent))
 
     def b1_copy(ds, dz):
         z2 = (zl + dz) % 2
         return (
             o_ref,
             g_ref.at[xi, 1 - ds, core, pl.ds(zl * B, B), :],
-            b1_send.at[ds + 1], b1_recv.at[1 - ds], dev(x, k, z2, y, s + ds),
+            sent, b1_recv.at[1 - ds], dev(x, k, z2, y, s + ds),
         )
 
     def b1_sends(ds):
@@ -148,9 +147,9 @@
                 taps = [w_ref[a * 9 + b * 3 + e] for b in range(3)]
                 wr_ref[core, slot, 0, a * 3 + e] = jnp.concatenate(
                     [t[:, h * B:(h + 1) * B] for t in taps] + [blank], axis=1)
-    w_across = (wr_ref.at[core, 2, 0], wr_ref.at[core, zl, 0], ws_send.at[0], ws_recv.at[0], dev(x, core, 1 - zl, y, s))
-    w_own = (wr_ref.at[core, zl], wr_ref.at[core, zl], ws_send.at[1], ws_recv.at[1], dev(x, other, zl, y, s))
-    w_next = (wr_ref.at[core, 1 - zl], wr_ref.at[core, 1 - zl], ws_send.at[2], ws_recv.at[2], dev(x, other, zl, y, s))
+    w_across = (wr_ref.at[core, 2, 0], wr_ref.at[core, zl, 0], sent, ws_recv.at[0], dev(x, core, 1 - zl, y, s))
+    w_own = (wr_ref.at[core, zl], wr_ref.at[core, zl], sent, ws_recv.at[1], dev(x, other, zl, y, s))
+    w_next = (wr_ref.at[core, 1 - zl], wr_ref.at[core, 1 - zl], sent, ws_recv.at[2], dev(x, other, zl, y, s))
     start(w_across)
 
     def turn(slot):
@@ -162,11 +161,11 @@
     @pl.when(has_high)
     def _():
         pl.semaphore_wait(up_sem, 4)
+        b1_sends(1)
         start(f1_copy(1))
-        b1_sends(1)
 
     def b2_copy(p, d):
-        return (g_ref.at[xi, p], g_ref.at[xi, p], b2_send.at[p], b2_recv.at[xi, p],
+        return (g_ref.at[xi, p], g_ref.at[xi, p], sent, b2_recv.at[xi, p],
                 dev((x + d) % NX, core, zl, y, s))
 
     def b2_sends(p):
@@ -202,13 +201,16 @@
     start(w_next)
 
     def low_g(p):
-        return (g_ref.at[0, p, 0, :, pl.ds(0, LANES)], hg_ref.at[p], h_send.at[p], h_recv.at[p], dev(x, other, zl, y, s))
+        return (g_ref.at[0, p, 0, :, pl.ds(0, LANES)], hg_ref.at[p], sent, h_recv.at[p], dev(x, other, zl, y, s))
 
     def high_g(p):
-        return (g_ref.at[1, p, 1, :, pl.ds(LANES, LANES)], hg_ref.at[p], h_send.at[p], h_recv.at[p], dev(x, other, zl, y, s))
-
-    low_d = (d_ref.at[0], hd_ref, h_send.at[3], h_recv.at[3], dev(x, other, zl, y, s))
-    high_d = (d_ref.at[NY - 1], hd_ref, h_send.at[3], h_recv.at[3], dev(x, other, zl, y, s))
+        return (g_ref.at[1, p, 1, :, pl.ds(LANES, LANES)], hg_ref.at[p], sent, h_recv.at[p], dev(x, other, zl, y, s))
+
+    def low_d(p):
+        return (d_ref.at[0, p], hd_ref.at[p], sent, h_recv.at[3 + p], dev(x, other, zl, y, s))
+
+    def high_d(p):
+        return (d_ref.at[NY - 1, p], hd_ref.at[p], sent, h_recv.at[3 + p], dev(x, other, zl, y, s))
 
     remote(*w_own).wait_recv()
     remote(*w_next).wait_recv()
@@ -276,7 +278,7 @@
             for dc in range(2):
                 c2 = (core + dc) % 2
                 start((pb_ref.at[t, pl.ds(c2 * B, B), :], rb_ref.at[y, pl.ds(zl * B, B), :],
-                       b3_send, b3_recv, dev(x, c2, core, t, s)),
+                       sent, b3_recv, dev(x, c2, core, t, s)),
                       jnp.logical_and(stays, y == t) if dc == 0 else None)
 
     for p in (1, 0, 2):
@@ -288,27 +290,29 @@
         pl.when(core == 0)(lambda: start(high_g(p)))
         pl.when(core == 1)(lambda: start(low_g(p)))
         rows(rg_ref, p, g_tile)
-    for pair in (1, 2):
+    for n, pair in enumerate((1,)):
         multiply(lb_ref, rg_ref, pair, emit_b)
-    got(d_ref.at[:, 1], f2_recv.at[1])
-    b3_sends((4, 3, 5, 2))
+        if n == 0:
+            got(d_ref.at[:, 1], f2_recv.at[1])
+        b3_sends((2 * pair, 2 * pair + 1))
     for p in range(3):
         got(hg_ref.at[p], h_recv.at[p])
         edge_rows(rg_ref, p, g_tile, hg_ref[p])
-    for pair in (0, 3):
+    for pair in (0, 3, 2):
         multiply(lb_ref, rg_ref, pair, emit_b)
-    b3_sends((0, 7, 1, 6))
+        b3_sends((2 * pair, 2 * pair + 1))
 
     def d_tile(a, t):
         return d_ref[t, a]
 
-    rows(rd_ref, 1, d_tile)
-    pl.when(has_low)(lambda: got(d_ref.at[:, 0], f2_recv.at[0]))
-    pl.when(has_high)(lambda: got(d_ref.at[:, 2], f2_recv.at[2]))
-    pl.when(core == 0)(lambda: start(high_d))
-    pl.when(core == 1)(lambda: start(low_d))
-    rows(rd_ref, 0, d_tile)
-    rows(rd_ref, 2, d_tile)
+    for p in (1, 0, 2):
+        if p == 0:
+            pl.when(has_low)(lambda: got(d_ref.at[:, 0], f2_recv.at[0]))
+        if p == 2:
+            pl.when(has_high)(lambda: got(d_ref.at[:, 2], f2_recv.at[2]))
+        pl.when(core == 0)(lambda: start(high_d(p)))
+        pl.when(core == 1)(lambda: start(low_d(p)))
+        rows(rd_ref, p, d_tile)
 
     def emit_f(t, total):
         for z in range(2):
@@ -318,26 +322,25 @@
         for dz in range(2):
             x2, c2, z2 = core * 2 + j // 2, j % 2, (zl + dz) % 2
             own = jnp.logical_and(x2 == x, c2 == core) if dz == 0 else None
-            start((pf_ref.at[j, z2], rf_ref.at[x, zl], f3_send, f3_recv, dev(x2, c2, z2, y, s)), own)
-
-    for pair in (1, 2):
+            start((pf_ref.at[j, z2], rf_ref.at[x, zl], sent, f3_recv, dev(x2, c2, z2, y, s)), own)
+
+    for pair in (1,):
         multiply(lf_ref, rd_ref, pair, emit_f)
         f3_sends(pair)
-    pl.when(core == 0)(lambda: remote(*low_d).wait_recv())
-    pl.when(core == 1)(lambda: remote(*high_d).wait_recv())
-    for a in range(3):
-        edge_rows(rd_ref, a, d_tile, hd_ref[a])
-    for pair in (0, 3):
+    for p in range(3):
+        got(hd_ref.at[p], h_recv.at[3 + p])
+        edge_rows(rd_ref, p, d_tile, hd_ref[p])
+    for pair in (0, 2, 3):
         multiply(lf_ref, rd_ref, pair, emit_f)
         f3_sends(pair)
 
     pl.when(has_low)(lambda: finish(f1_copy(-1)))
     pl.when(has_high)(lambda: finish(f1_copy(1)))
     pair = g_ref.at[0, 0, 0]
-    pl.when(has_low)(lambda: got(pair, b1_send.at[0]))
-    pl.when(has_high)(lambda: got(pair, b1_send.at[2]))
-    pl.when(relay)(lambda: got(pair.at[pl.ds(0, B)], b1_send.at[1]))
-    pl.when(jnp.logical_not(relay))(lambda: got(pair, b1_send.at[1]))
+    pl.when(has_low)(lambda: got(pair, sent))
+    pl.when(has_high)(lambda: got(pair, sent))
+    pl.when(relay)(lambda: got(pair.at[pl.ds(0, B)], sent))
+    pl.when(jnp.logical_not(relay))(lambda: got(pair, sent))
     f2_finish(1)
     pl.when(has_low)(lambda: f2_finish(0))
     pl.when(has_high)(lambda: f2_finish(2))
@@ -347,18 +350,18 @@
     @pl.when(relay)
     def _():
         for p in range(3):
-            got(g_ref.at[0], b2_send.at[p])
+            got(g_ref.at[0], sent)
 
     for p in range(3):
-        got(hg_ref.at[p], h_send.at[p])
-    pl.when(core == 0)(lambda: finish(high_d))
-    pl.when(core == 1)(lambda: finish(low_d))
-    got(pb_ref.at[pl.ds(0, NY - 1)], b3_send)
-    got(pb_ref.at[NY - 1, pl.ds(0, B)], b3_send)
-    pl.when(jnp.logical_not(stays))(lambda: got(pb_ref.at[NY - 1, pl.ds(B, B)], b3_send))
-    got(pf_ref.at[pl.ds(0, NX - 1)], f3_send)
-    got(pf_ref.at[NX - 1, 0], f3_send)
-    pl.when(jnp.logical_not(relay))(lambda: got(pf_ref.at[NX - 1, 1], f3_send))
+        got(hg_ref.at[p], sent)
+    for p in range(3):
+        got(hd_ref.at[p], sent)
+    got(pb_ref.at[pl.ds(0, NY - 1)], sent)
+    got(pb_ref.at[NY - 1, pl.ds(0, B)], sent)
+    pl.when(jnp.logical_not(stays))(lambda: got(pb_ref.at[NY - 1, pl.ds(B, B)], sent))
+    got(pf_ref.at[pl.ds(0, NX - 1)], sent)
+    got(pf_ref.at[NX - 1, 0], sent)
+    pl.when(jnp.logical_not(relay))(lambda: got(pf_ref.at[NX - 1, 1], sent))
 
     got(rf_ref, f3_recv)
     total = rf_ref[0, 0]
@@ -407,14 +410,8 @@
                 pltpu.VMEM((NX, 2, B, wide), F32),
                 pltpu.VMEM((NY, 2 * B, LANES), F32),
                 pltpu.VMEM((NX, 2, B, wide), F32),
-                dma((3,)),
-                dma((2,)), dma((2,)),
-                dma((3,)), dma((3,)),
-                dma((3,)), dma((3,)),
-                dma((3,)), dma((2, 3)),
-                dma((3,)), dma((3,)),
-                dma((4,)), dma((4,)),
-                dma, dma,
+                dma((3,)), dma,
+                dma((2,)), dma((3,)), dma((3,)), dma((2, 3)), dma((3,)), dma((6,)),
                 dma, dma,
                 pltpu.SemaphoreType.REGULAR,
             ],

time: 33.7 us -> 33 us (0.979)
  the two profiles are of different devices: /device:TPU:384 before, /device:TPU:395 now
where the time goes in v5:
time: 33 us; the launch traced here: 32.8 us
  Pallas kernels  30.9 us (94%)
  local copies, waits for them, and re-layouts  1.21 us (4%)
  between operations  0.64 us (2%)
    pallas_call x1, Pallas kernels, local(): pl.pallas_call(functools.partial(kernel, ns), out_shape=(pltpu.VMEM((B, w...  30.9 us
    unnamed x2, local copies, waits for them, and re-layouts  1.21 us

profile of v5, /device:TPU:395, one launch (start us, length us, event | category | flops | bytes accessed | tf_op | source)
XLA Modules:
  0.0 32.8 jit_solution(4052390959310579582)
XLA Ops:
  0.6 30.9 %shard_map.50 = (bf16[32,256]{1,0:T(8,128)(2,1)S(1)}, bf16[64,128]{1,0:T(8,128)(2,1)S(1)}) custom-call(bf16[64,128]{1,0:T(8,128)(2,1)} %bitcast.10, bf16[27,32,64]{2,1,0:T(8,128)(2,1)} %bitcast.9, bf16[32,256]{1,0:T(8,128)(2,1)} %bitcast.11), custom_call_target="tpu_custom_call" | custom-call | tf_op jit(solution)/shard_map/pallas_call | solution.py:388
  31.6 0.6 %copy.7 = bf16[32,1,256]{2,0,1:T(8,128)(2,1)} copy(bf16[32,1,256]{2,0,1:T(8,128)(2,1)S(1)} %bitcast.8) | data formatting | bytes 32768
  32.2 0.6 %copy.8 = bf16[64,1,128]{2,0,1:T(8,128)(2,1)} copy(bf16[64,1,128]{2,0,1:T(8,128)(2,1)S(1)} %bitcast.7) | data formatting | bytes 32768

commit v6 on v5

--- a/solution.py
+++ b/solution.py
@@ -13,6 +13,7 @@
 B = 32
 NX, NY = 4, 8
 FAR = (4, 3, 5, 2, 6, 1, 7)
+ORDER = (0, 1, 7, 2, 6, 3, 5, 4)
 LANES = 128
 
 
@@ -63,15 +64,14 @@
         pl.semaphore_signal(sem, inc=1, device_id=to, device_id_type=MESH)
 
     loads = [
-        pltpu.make_async_copy(act_hbm, a_ref.at[1], load_sem.at[0]),
+        pltpu.make_async_copy(act_hbm, a_ref, load_sem.at[0]),
         pltpu.make_async_copy(og_hbm, o_ref, load_sem.at[1]),
         pltpu.make_async_copy(w_hbm, w_ref, load_sem.at[2]),
     ]
     for load in loads:
         load.start()
     for d in FAR:
-        for c in range(2):
-            greet(dev(x, c, core, (y + d) % NY, s))
+        greet(dev(x, core, zl, (y + d) % NY, s))
 
     def greet_slab(ds):
         for dc in range(2):
@@ -95,7 +95,7 @@
     pl.when(jnp.logical_not(has_high))(lambda: clear_planes(2))
     loads[0].wait()
     loads[1].wait()
-    count = 2 * (NY - 1) + 3 + (NX - 1)
+    count = (NY - 1) + 3 + (NX - 1)
     pl.semaphore_wait(barrier, count + 4 * has_low.astype(jnp.int32))
 
     @pl.when(has_low)
@@ -104,22 +104,18 @@
             for dz in range(2):
                 greet(dev(x, (core + dc) % 2, (zl + dz) % 2, y, s - 1), up_sem)
 
-    def f1_copy(ds):
-        return (a_ref.at[1], a_ref.at[1 - ds], sent, f1_recv.at[(1 - ds) // 2],
-                dev(x, core, zl, y, s + ds))
-
-    def f2_sends(p, across):
-        for y2 in (0, 1, 7, 2, 6, 3, 5, 4):
-            for dz in across:
-                z2 = (zl + dz) % 2
-                start((a_ref.at[p, pl.ds(z2 * B, B), :], d_ref.at[y, p, pl.ds(core * B, B), :],
-                       sent, f2_recv.at[p], dev(x, zl, z2, y2, s)),
-                      jnp.logical_and(stays, y == y2) if dz == 0 else None)
-
-    def f2_finish(p):
-        got(d_ref.at[pl.ds(0, NY - 1), p], sent)
-        got(d_ref.at[NY - 1, p, pl.ds(0, B)], sent)
-        pl.when(jnp.logical_not(stays))(lambda: got(d_ref.at[NY - 1, p, pl.ds(B, B)], sent))
+    def f1_sends(ds):
+        for dz in range(2):
+            z2 = (zl + dz) % 2
+            start((a_ref.at[pl.ds(z2 * B, B), :], d_ref.at[y, 1 - ds, pl.ds(core * B, B), :],
+                   sent, f1_recv.at[1 - ds], dev(x, zl, z2, y, s + ds)),
+                  stays if (ds, dz) == (0, 0) else None)
+
+    def f2_sends(p):
+        for y2 in ORDER:
+            @pl.when(y != y2)
+            def _(y2=y2):
+                start((d_ref.at[y, p], d_ref.at[y, p], sent, f2_recv.at[p], dev(x, core, zl, y2, s)))
 
     def b1_copy(ds, dz):
         z2 = (zl + dz) % 2
@@ -133,10 +129,10 @@
         for dz in range(2):
             start(b1_copy(ds, dz), relay if (ds, dz) == (0, 0) else None)
 
-    pl.when(has_low)(lambda: start(f1_copy(-1)))
+    pl.when(has_low)(lambda: f1_sends(-1))
     pl.when(has_low)(lambda: b1_sends(-1))
+    f1_sends(0)
     b1_sends(0)
-    f2_sends(1, (0, 1))
 
     loads[2].wait()
     blank = jnp.zeros((B, B), BF16)
@@ -151,6 +147,8 @@
     w_own = (wr_ref.at[core, zl], wr_ref.at[core, zl], sent, ws_recv.at[1], dev(x, other, zl, y, s))
     w_next = (wr_ref.at[core, 1 - zl], wr_ref.at[core, 1 - zl], sent, ws_recv.at[2], dev(x, other, zl, y, s))
     start(w_across)
+    got(d_ref.at[y, 1], f1_recv.at[1])
+    f2_sends(1)
 
     def turn(slot):
         for i in range(9):
@@ -162,7 +160,7 @@
     def _():
         pl.semaphore_wait(up_sem, 4)
         b1_sends(1)
-        start(f1_copy(1))
+        f1_sends(1)
 
     def b2_copy(p, d):
         return (g_ref.at[xi, p], g_ref.at[xi, p], sent, b2_recv.at[xi, p],
@@ -179,13 +177,13 @@
 
     @pl.when(has_low)
     def _():
-        got(a_ref.at[0], f1_recv.at[0])
-        f2_sends(0, (0, 1))
+        got(d_ref.at[y, 0], f1_recv.at[0])
+        f2_sends(0)
 
     @pl.when(has_high)
     def _():
-        got(a_ref.at[2], f1_recv.at[1])
-        f2_sends(2, (0, 1))
+        got(d_ref.at[y, 2], f1_recv.at[2])
+        f2_sends(2)
 
     @pl.when(relay)
     def _():
@@ -290,11 +288,9 @@
         pl.when(core == 0)(lambda: start(high_g(p)))
         pl.when(core == 1)(lambda: start(low_g(p)))
         rows(rg_ref, p, g_tile)
-    for n, pair in enumerate((1,)):
-        multiply(lb_ref, rg_ref, pair, emit_b)
-        if n == 0:
-            got(d_ref.at[:, 1], f2_recv.at[1])
-        b3_sends((2 * pair, 2 * pair + 1))
+    multiply(lb_ref, rg_ref, 1, emit_b)
+    got(d_ref.at[pl.ds(0, NY - 1), 1], f2_recv.at[1])
+    b3_sends((2, 3))
     for p in range(3):
         got(hg_ref.at[p], h_recv.at[p])
         edge_rows(rg_ref, p, g_tile, hg_ref[p])
@@ -307,9 +303,9 @@
 
     for p in (1, 0, 2):
         if p == 0:
-            pl.when(has_low)(lambda: got(d_ref.at[:, 0], f2_recv.at[0]))
+            pl.when(has_low)(lambda: got(d_ref.at[pl.ds(0, NY - 1), 0], f2_recv.at[0]))
         if p == 2:
-            pl.when(has_high)(lambda: got(d_ref.at[:, 2], f2_recv.at[2]))
+            pl.when(has_high)(lambda: got(d_ref.at[pl.ds(0, NY - 1), 2], f2_recv.at[2]))
         pl.when(core == 0)(lambda: start(high_d(p)))
         pl.when(core == 1)(lambda: start(low_d(p)))
         rows(rd_ref, p, d_tile)
@@ -334,16 +330,18 @@
         multiply(lf_ref, rd_ref, pair, emit_f)
         f3_sends(pair)
 
-    pl.when(has_low)(lambda: finish(f1_copy(-1)))
-    pl.when(has_high)(lambda: finish(f1_copy(1)))
+    pl.when(has_low)(lambda: got(a_ref, sent))
+    pl.when(has_high)(lambda: got(a_ref, sent))
+    got(a_ref.at[pl.ds(0, B)], sent)
+    pl.when(jnp.logical_not(stays))(lambda: got(a_ref.at[pl.ds(B, B)], sent))
     pair = g_ref.at[0, 0, 0]
     pl.when(has_low)(lambda: got(pair, sent))
     pl.when(has_high)(lambda: got(pair, sent))
     pl.when(relay)(lambda: got(pair.at[pl.ds(0, B)], sent))
     pl.when(jnp.logical_not(relay))(lambda: got(pair, sent))
-    f2_finish(1)
-    pl.when(has_low)(lambda: f2_finish(0))
-    pl.when(has_high)(lambda: f2_finish(2))
+    got(d_ref.at[pl.ds(0, NY - 1), 1], sent)
+    pl.when(has_low)(lambda: got(d_ref.at[pl.ds(0, NY - 1), 0], sent))
+    pl.when(has_high)(lambda: got(d_ref.at[pl.ds(0, NY - 1), 2], sent))
     for copy in (w_across, w_own, w_next):
         finish(copy)
 
@@ -394,7 +392,7 @@
             in_specs=[pl.BlockSpec(memory_space=pl.ANY)] * 3,
             out_specs=(pl.BlockSpec(memory_space=pltpu.VMEM),) * 2,
             scratch_shapes=[
-                pltpu.VMEM((3, 2 * B, LANES), BF16),
+                pltpu.VMEM((2 * B, LANES), BF16),
                 pltpu.VMEM((B, wide), BF16),
                 pltpu.VMEM((27, B, 2 * B), BF16),
                 pltpu.VMEM((NY, 3, 2 * B, LANES), BF16),
@@ -411,7 +409,7 @@
                 pltpu.VMEM((NY, 2 * B, LANES), F32),
                 pltpu.VMEM((NX, 2, B, wide), F32),
                 dma((3,)), dma,
-                dma((2,)), dma((3,)), dma((3,)), dma((2, 3)), dma((3,)), dma((6,)),
+                dma((3,)), dma((3,)), dma((3,)), dma((2, 3)), dma((3,)), dma((6,)),
                 dma, dma,
                 pltpu.SemaphoreType.REGULAR,
             ],

time: 33 us -> 32.5 us (0.985)
  the two profiles are of different devices: /device:TPU:395 before, /device:TPU:387 now
where the time goes in v6:
time: 32.5 us; the launch traced here: 32.3 us
  Pallas kernels  30.5 us (94%)
  local copies, waits for them, and re-layouts  1.21 us (4%)
  between operations  0.64 us (2%)
    pallas_call x1, Pallas kernels, local(): pl.pallas_call(functools.partial(kernel, ns), out_shape=(pltpu.VMEM((B, w...  30.5 us
    unnamed x2, local copies, waits for them, and re-layouts  1.21 us

profile of v6, /device:TPU:387, one launch (start us, length us, event | category | flops | bytes accessed | tf_op | source)
XLA Modules:
  0.0 32.3 jit_solution(1853165656018153621)
XLA Ops:
  0.6 30.5 %shard_map.50 = (bf16[32,256]{1,0:T(8,128)(2,1)S(1)}, bf16[64,128]{1,0:T(8,128)(2,1)S(1)}) custom-call(bf16[64,128]{1,0:T(8,128)(2,1)} %bitcast.10, bf16[27,32,64]{2,1,0:T(8,128)(2,1)} %bitcast.9, bf16[32,256]{1,0:T(8,128)(2,1)} %bitcast.11), custom_call_target="tpu_custom_call" | custom-call | tf_op jit(solution)/shard_map/pallas_call | solution.py:386
  31.1 0.6 %copy.7 = bf16[32,1,256]{2,0,1:T(8,128)(2,1)} copy(bf16[32,1,256]{2,0,1:T(8,128)(2,1)S(1)} %bitcast.8) | data formatting | bytes 32768
  31.7 0.6 %copy.8 = bf16[64,1,128]{2,0,1:T(8,128)(2,1)} copy(bf16[64,1,128]{2,0,1:T(8,128)(2,1)S(1)} %bitcast.7) | data formatting | bytes 32768

commit v7 on v6

--- a/solution.py
+++ b/solution.py
@@ -84,12 +84,15 @@
     for d in range(1, NX):
         greet(dev((x + d) % NX, core, zl, y, s))
 
+    def inside(p, body):
+        if p == 1:
+            body()
+        else:
+            pl.when(has_low if p == 0 else has_high)(body)
+
     def clear_planes(p):
-        d_ref[:, p] = jnp.zeros((NY,) + d_ref.shape[2:], BF16)
-
-        @pl.when(relay)
-        def _():
-            g_ref[xi, p] = jnp.zeros(g_ref.shape[2:], BF16)
+        for r_ref in (rg_ref, rd_ref):
+            r_ref[p * 256:(p + 1) * 256, :] = jnp.zeros((256, r_ref.shape[1]), BF16)
 
     pl.when(jnp.logical_not(has_low))(lambda: clear_planes(0))
     pl.when(jnp.logical_not(has_high))(lambda: clear_planes(2))
@@ -185,12 +188,11 @@
         got(d_ref.at[y, 2], f1_recv.at[2])
         f2_sends(2)
 
-    @pl.when(relay)
-    def _():
-        pl.when(has_low)(lambda: got(g_ref.at[xi, 0], b1_recv.at[0]))
-        b2_sends(0)
-        pl.when(has_high)(lambda: got(g_ref.at[xi, 2], b1_recv.at[2]))
-        b2_sends(2)
+    for p, has in ((0, has_low), (2, has_high)):
+        @pl.when(jnp.logical_and(relay, has))
+        def _(p=p):
+            got(g_ref.at[xi, p], b1_recv.at[p])
+            b2_sends(p)
 
     turn(zl)
     start(w_own)
@@ -279,21 +281,25 @@
                        sent, b3_recv, dev(x, c2, core, t, s)),
                       jnp.logical_and(stays, y == t) if dc == 0 else None)
 
-    for p in (1, 0, 2):
+    def g_plane(p):
         for i in range(2):
-            @pl.when(jnp.logical_not(jnp.logical_and(relay, xi == i)))
-            def _(i=i, p=p):
-                got(g_ref.at[i, p], b2_recv.at[i, p])
-
+            pl.when(jnp.logical_not(jnp.logical_and(relay, xi == i)))(
+                lambda i=i: got(g_ref.at[i, p], b2_recv.at[i, p]))
         pl.when(core == 0)(lambda: start(high_g(p)))
         pl.when(core == 1)(lambda: start(low_g(p)))
         rows(rg_ref, p, g_tile)
+
+    def g_edges(p):
+        got(hg_ref.at[p], h_recv.at[p])
+        edge_rows(rg_ref, p, g_tile, hg_ref[p])
+
+    for p in (1, 0, 2):
+        inside(p, functools.partial(g_plane, p))
     multiply(lb_ref, rg_ref, 1, emit_b)
     got(d_ref.at[pl.ds(0, NY - 1), 1], f2_recv.at[1])
     b3_sends((2, 3))
     for p in range(3):
-        got(hg_ref.at[p], h_recv.at[p])
-        edge_rows(rg_ref, p, g_tile, hg_ref[p])
+        inside(p, functools.partial(g_edges, p))
     for pair in (0, 3, 2):
         multiply(lb_ref, rg_ref, pair, emit_b)
         b3_sends((2 * pair, 2 * pair + 1))
@@ -301,14 +307,19 @@
     def d_tile(a, t):
         return d_ref[t, a]
 
-    for p in (1, 0, 2):
-        if p == 0:
-            pl.when(has_low)(lambda: got(d_ref.at[pl.ds(0, NY - 1), 0], f2_recv.at[0]))
-        if p == 2:
-            pl.when(has_high)(lambda: got(d_ref.at[pl.ds(0, NY - 1), 2], f2_recv.at[2]))
+    def d_plane(p):
+        if p != 1:
+            got(d_ref.at[pl.ds(0, NY - 1), p], f2_recv.at[p])
         pl.when(core == 0)(lambda: start(high_d(p)))
         pl.when(core == 1)(lambda: start(low_d(p)))
         rows(rd_ref, p, d_tile)
+
+    def d_edges(p):
+        got(hd_ref.at[p], h_recv.at[3 + p])
+        edge_rows(rd_ref, p, d_tile, hd_ref[p])
+
+    for p in (1, 0, 2):
+        inside(p, functools.partial(d_plane, p))
 
     def emit_f(t, total):
         for z in range(2):
@@ -324,8 +335,7 @@
         multiply(lf_ref, rd_ref, pair, emit_f)
         f3_sends(pair)
     for p in range(3):
-        got(hd_ref.at[p], h_recv.at[3 + p])
-        edge_rows(rd_ref, p, d_tile, hd_ref[p])
+        inside(p, functools.partial(d_edges, p))
     for pair in (0, 2, 3):
         multiply(lf_ref, rd_ref, pair, emit_f)
         f3_sends(pair)
@@ -348,12 +358,11 @@
     @pl.when(relay)
     def _():
         for p in range(3):
-            got(g_ref.at[0], sent)
+            inside(p, lambda: got(g_ref.at[0], sent))
 
     for p in range(3):
-        got(hg_ref.at[p], sent)
-    for p in range(3):
-        got(hd_ref.at[p], sent)
+        inside(p, lambda p=p: got(hg_ref.at[p], sent))
+        inside(p, lambda p=p: got(hd_ref.at[p], sent))
     got(pb_ref.at[pl.ds(0, NY - 1)], sent)
     got(pb_ref.at[NY - 1, pl.ds(0, B)], sent)
     pl.when(jnp.logical_not(stays))(lambda: got(pb_ref.at[NY - 1, pl.ds(B, B)], sent))

time: 32.5 us -> 32.7 us (level)
  the two profiles are of different devices: /device:TPU:387 before, /device:TPU:259 now
where the time goes in v7:
time: 32.7 us; the launch traced here: 32.5 us
  Pallas kernels  30.6 us (94%)
  local copies, waits for them, and re-layouts  1.21 us (4%)
  between operations  0.64 us (2%)
    pallas_call x1, Pallas kernels, local(): pl.pallas_call(functools.partial(kernel, ns), out_shape=(pltpu.VMEM((B, w...  30.6 us
    unnamed x2, local copies, waits for them, and re-layouts  1.21 us

profile of v7, /device:TPU:259, one launch (start us, length us, event | category | flops | bytes accessed | tf_op | source)
XLA Modules:
  0.0 32.5 jit_solution(9602961247403186261)
XLA Ops:
  0.6 30.6 %shard_map.50 = (bf16[32,256]{1,0:T(8,128)(2,1)S(1)}, bf16[64,128]{1,0:T(8,128)(2,1)S(1)}) custom-call(bf16[64,128]{1,0:T(8,128)(2,1)} %bitcast.10, bf16[27,32,64]{2,1,0:T(8,128)(2,1)} %bitcast.9, bf16[32,256]{1,0:T(8,128)(2,1)} %bitcast.11), custom_call_target="tpu_custom_call" | custom-call | tf_op jit(solution)/shard_map/pallas_call | solution.py:395
  31.3 0.6 %copy.7 = bf16[32,1,256]{2,0,1:T(8,128)(2,1)} copy(bf16[32,1,256]{2,0,1:T(8,128)(2,1)S(1)} %bitcast.8) | data formatting | bytes 32768
  31.9 0.6 %copy.8 = bf16[64,1,128]{2,0,1:T(8,128)(2,1)} copy(bf16[64,1,128]{2,0,1:T(8,128)(2,1)S(1)} %bitcast.7) | data formatting | bytes 32768

commit v8 on v7

--- a/solution.py
+++ b/solution.py
@@ -293,7 +293,7 @@
         got(hg_ref.at[p], h_recv.at[p])
         edge_rows(rg_ref, p, g_tile, hg_ref[p])
 
-    for p in (1, 0, 2):
+    for p in (1, 2, 0):
         inside(p, functools.partial(g_plane, p))
     multiply(lb_ref, rg_ref, 1, emit_b)
     got(d_ref.at[pl.ds(0, NY - 1), 1], f2_recv.at[1])
@@ -318,7 +318,7 @@
         got(hd_ref.at[p], h_recv.at[3 + p])
         edge_rows(rd_ref, p, d_tile, hd_ref[p])
 
-    for p in (1, 0, 2):
+    for p in (1, 2, 0):
         inside(p, functools.partial(d_plane, p))
 
     def emit_f(t, total):

time: 32.7 us -> 32.7 us (level)
  the two profiles are of different devices: /device:TPU:259 before, /device:TPU:267 now
where the time goes in v8:
time: 32.7 us; the launch traced here: 32.5 us
  Pallas kernels  30.6 us (94%)
  local copies, waits for them, and re-layouts  1.21 us (4%)
  between operations  0.64 us (2%)
    pallas_call x1, Pallas kernels, local(): pl.pallas_call(functools.partial(kernel, ns), out_shape=(pltpu.VMEM((B, w...  30.6 us
    unnamed x2, local copies, waits for them, and re-layouts  1.21 us

profile of v8, /device:TPU:267, one launch (start us, length us, event | category | flops | bytes accessed | tf_op | source)
XLA Modules:
  0.0 32.5 jit_solution(12883828673835619908)
XLA Ops:
  0.6 30.6 %shard_map.50 = (bf16[32,256]{1,0:T(8,128)(2,1)S(1)}, bf16[64,128]{1,0:T(8,128)(2,1)S(1)}) custom-call(bf16[64,128]{1,0:T(8,128)(2,1)} %bitcast.10, bf16[27,32,64]{2,1,0:T(8,128)(2,1)} %bitcast.9, bf16[32,256]{1,0:T(8,128)(2,1)} %bitcast.11), custom_call_target="tpu_custom_call" | custom-call | tf_op jit(solution)/shard_map/pallas_call | solution.py:395
  31.3 0.6 %copy.7 = bf16[32,1,256]{2,0,1:T(8,128)(2,1)} copy(bf16[32,1,256]{2,0,1:T(8,128)(2,1)S(1)} %bitcast.8) | data formatting | bytes 32768
  31.9 0.6 %copy.8 = bf16[64,1,128]{2,0,1:T(8,128)(2,1)} copy(bf16[64,1,128]{2,0,1:T(8,128)(2,1)S(1)} %bitcast.7) | data formatting | bytes 32768
